TPU v7x, 256 devices: a whole 4x4x8 slice. The times are simulated.
256 devices in a mesh: sta: 8 (over x, core), cel: 32 (over z, y).
Axes of the slice: x: 4, y: 4, z: 8, core: 2. Of those that a mesh axis runs over, the one named last changes fastest.
Arguments:
- model_vectors: bfloat16 [16, 262144], P('sta', 'cel'), may hold values from -6 to 6
- station_xyz: float32 [3, 262144], P(None, 'sta'), may hold values from 0 to 2, as said below
- cell_xyz: float32 [3, 262144], P(None, 'cel'), may hold values from -1 to 2, as said below
- weights: float32 [262144], P('sta'), may hold values from 0.25 to 4
- near_pairs: int32 [8, 32, 64, 2], P('sta', 'cel'), may hold values from 0 to 127, as said below
- near_count: int32 [8, 32], P('sta'), may hold values from 8 to 64, as said below
- mid_pairs: int32 [8, 32, 128, 2], P('sta', 'cel'), may hold values from 0 to 127, as said below
- mid_u: bfloat16 [8, 32, 128, 32, 256], P('sta', 'cel'), may hold values from -0.375 to 0.375
- mid_v: bfloat16 [8, 32, 128, 32, 256], P('sta', 'cel'), may hold values from -0.375 to 0.375
Outputs:
- predicted: float32 [16, 262144], P(None, ('sta', 'cel'))
- gradient: float32 [16, 262144], P('sta', 'cel')
Inputs may be any that keep to these rules, and one draw needn't show every extreme that they name: `near_pairs`: entry 0 of a pair is a station tile below 128, entry 1 a cell tile below 32; a device's near and mid pairs are all different; slots at or past the device's near_count are ignored. `mid_pairs`: entry 0 a station tile below 128, entry 1 a cell tile below 32. `near_count`: each count is 64 divided by 1, 2, 4 or 8; some device has 64. `station_xyz`: east and north lie in 0 to 2; heights in 0.5 to 1. `cell_xyz`: east and north lie in 0 to 2; heights in -1 to -0.25.
All inputs are finite; a program needn't handle non-finite values.
Results may differ from a plain program's by a relative error of at most 0.015.
Values may be sent and summed in bfloat16 or wider, within the bound.
No kernel may reach another device: no remote copies, remote signals or barrier semaphores. Data moves between devices by JAX's collectives and lax.ppermute only.
A program may use at most 128 MiB of HBM per device.

v0:
```python
import jax
import jax.numpy as jnp
from jax import lax
from jax.sharding import PartitionSpec as P

VOLUME = 0.03125
FIELD_X = 0.17101
FIELD_Y = 0.46985
FIELD_Z = -0.86603


def kernel_group(stations, cell_points):
    delta_x = stations[0][:, None, :] - cell_points[0][:, :, None]
    delta_y = stations[1][:, None, :] - cell_points[1][:, :, None]
    delta_z = stations[2][:, None, :] - cell_points[2][:, :, None]
    inverse = lax.rsqrt(delta_x * delta_x + delta_y * delta_y + delta_z * delta_z)
    aligned = (FIELD_X * delta_x + FIELD_Y * delta_y + FIELD_Z * delta_z) * inverse
    return (VOLUME * (3.0 * aligned * aligned - 1.0) * inverse * inverse * inverse).astype(
        jnp.bfloat16
    )


def group_width():
    return 8


def build_group(station_grid, slot_rows, slot_cells, first, width):
    rows_here = lax.dynamic_slice_in_dim(slot_rows, first, width)
    stations = jnp.take(station_grid, rows_here, axis=1)
    cells_here = lax.dynamic_slice_in_dim(slot_cells, first, width, 1)
    return (rows_here, kernel_group(stations, cells_here))


def forward_pass(live_total, slot_rows, slot_cells, slot_vectors, station_grid, totals):
    tile_size = totals.shape[2]
    station_tiles = totals.shape[1]
    width = group_width()
    stored = jnp.zeros((1, tile_size, tile_size), jnp.bfloat16)
    station_range = jnp.arange(station_tiles, dtype=jnp.int32)
    turns = (live_total + width - 1) // width

    def forward_advance(group_index, loop_state):
        running, kept = loop_state
        first = group_index * width
        rows_here, kernel_blocks = build_group(station_grid, slot_rows, slot_cells, first, width)
        live = first + jnp.arange(width, dtype=jnp.int32) < live_total
        source = lax.dynamic_slice_in_dim(slot_vectors, first, width, 1)
        terms = jnp.einsum(
            "vbc,bcs->vbs", source, kernel_blocks, preferred_element_type=jnp.float32
        )
        row_hot = ((rows_here[:, None] == station_range[None, :]) & live[:, None]).astype(
            jnp.float32
        )
        running = running + jnp.einsum(
            "vbs,bt->vts", terms, row_hot, precision=lax.Precision.HIGHEST
        )
        return (running, kept)

    return lax.fori_loop(0, turns, forward_advance, (totals, stored))


def adjoint_pass(live_total, slot_rows, slot_cells, station_grid, data_tiles, slot_terms):
    width = group_width()
    turns = (live_total + width - 1) // width

    def adjoint_advance(group_index, running):
        first = group_index * width
        rows_here = lax.dynamic_slice_in_dim(slot_rows, first, width)
        rows_here, kernel_blocks = build_group(station_grid, slot_rows, slot_cells, first, width)
        live = first + jnp.arange(width, dtype=jnp.int32) < live_total
        data_here = jnp.take(data_tiles, rows_here, axis=1)
        terms = jnp.einsum(
            "vbs,bcs->vbc", data_here, kernel_blocks, preferred_element_type=jnp.float32
        )
        terms = jnp.where(live[None, :, None], terms, 0.0)
        return lax.dynamic_update_slice_in_dim(running, terms, first, 1)

    return lax.fori_loop(0, turns, adjoint_advance, slot_terms)


def body(
    model_vectors, station_xyz, cell_xyz, weights, near_pairs, near_count, mid_pairs, mid_u, mid_v
):
    tile_size = mid_u.shape[-1]
    station_tiles = station_xyz.shape[1] // tile_size
    cell_tiles = cell_xyz.shape[1] // tile_size
    vectors = lax.all_gather(model_vectors, "sta", axis=0, tiled=True)
    vec_count = vectors.shape[0]
    vector_tiles = vectors.reshape(vec_count, cell_tiles, tile_size)
    station_grid = station_xyz.reshape(3, station_tiles, tile_size)
    cell_grid = cell_xyz.reshape(3, cell_tiles, tile_size)
    near_list = near_pairs[0, 0]
    near_slots = near_list.shape[0]
    near_rows = near_list[:, 0]
    near_columns = near_list[:, 1]
    cel_index = lax.axis_index("cel")
    own_count = near_count[0, cel_index]
    station_range = jnp.arange(station_tiles, dtype=jnp.int32)
    cell_range = jnp.arange(cell_tiles, dtype=jnp.int32)
    mid_list = mid_pairs[0, 0]
    mid_rows = mid_list[:, 0]
    mid_columns = mid_list[:, 1]
    u_factor = mid_u[0, 0]
    v_factor = mid_v[0, 0]
    row_hot = (mid_rows[:, None] == station_range[None, :]).astype(jnp.float32)
    column_hot = (mid_columns[:, None] == cell_range[None, :]).astype(jnp.float32)
    picked = jnp.take(vector_tiles, mid_columns, axis=1)
    reduced = jnp.einsum(
        "vmc,mrc->vmr", picked, v_factor, preferred_element_type=jnp.float32
    ).astype(jnp.bfloat16)
    spread = jnp.einsum("vmr,mrs->vms", reduced, u_factor, preferred_element_type=jnp.float32)
    forward_sum = jnp.einsum("vms,mt->vts", spread, row_hot, precision=lax.Precision.HIGHEST)
    own_cells = jnp.take(cell_grid, near_columns, axis=1)
    own_vectors = jnp.take(vector_tiles, near_columns, axis=1)
    forward_sum, own_stored = forward_pass(
        own_count, near_rows, own_cells, own_vectors, station_grid, forward_sum
    )
    partial_data = forward_sum.reshape(vec_count, station_tiles * tile_size)
    share = partial_data.shape[1] // lax.axis_size("cel")
    predicted = lax.psum_scatter(partial_data, "cel", scatter_dimension=1, tiled=True)
    weight_share = lax.dynamic_slice_in_dim(weights, cel_index * share, share)
    weighted_share = (predicted * weight_share[None, :]).astype(jnp.bfloat16)
    weighted = lax.all_gather(weighted_share, "cel", axis=1, tiled=True)
    data_tiles = weighted.reshape(vec_count, station_tiles, tile_size)
    fetched = jnp.take(data_tiles, mid_rows, axis=1)
    pulled = jnp.einsum(
        "vms,mrs->vmr", fetched, u_factor, preferred_element_type=jnp.float32
    ).astype(jnp.bfloat16)
    expanded = jnp.einsum("vmr,mrc->vmc", pulled, v_factor, preferred_element_type=jnp.float32)
    adjoint_sum = jnp.einsum("vmc,mt->vtc", expanded, column_hot, precision=lax.Precision.HIGHEST)
    own_terms = adjoint_pass(
        own_count,
        near_rows,
        own_cells,
        station_grid,
        data_tiles,
        jnp.zeros((vec_count, near_slots, tile_size), jnp.float32),
    )
    near_hot = (near_columns[:, None] == cell_range[None, :]).astype(jnp.float32)
    adjoint_sum = adjoint_sum + jnp.einsum(
        "vkc,kt->vtc", own_terms, near_hot, precision=lax.Precision.HIGHEST
    )
    gradient = lax.psum_scatter(
        adjoint_sum.reshape(vec_count, cell_tiles * tile_size).astype(jnp.bfloat16),
        "sta",
        scatter_dimension=0,
        tiled=True,
    ).astype(jnp.float32)
    return (predicted, gradient)


def solution(mesh):
    return jax.shard_map(
        body,
        mesh=mesh,
        in_specs=(
            P("sta", "cel"),
            P(None, "sta"),
            P(None, "cel"),
            P("sta"),
            P("sta", "cel", None, None),
            P("sta", None),
            P("sta", "cel", None, None),
            P("sta", "cel", None, None, None),
            P("sta", "cel", None, None, None),
        ),
        out_specs=(P(None, ("sta", "cel")), P("sta", "cel")),
        check_vma=False,
    )
```

profile of v0, /device:TPU:1, one launch (start us, length us, event | category | flops | bytes accessed | tf_op | source)
XLA Modules:
  0.0 557.6 jit_solution(2480626685229786508)
XLA Ops:
  7.2 1.4 slice_bitcast_fusion.2
  8.6 1.3 and_bitcast_fusion
  10.0 1.3 constant_dynamic-slice_fusion
  11.9 1.3 slice_bitcast_fusion.1
  13.2 0.7 and_bitcast_fusion.1
  13.9 16.1 %all-gather = bf16[8,2,8192]{2,1,0:T(2,128)(2,1)S(1)} all-gather(bf16[1,2,8192]{2,1,0:T(2,128)(2,1)} %bitcast.188), channel_id=1, replica_groups=mesh['sta'=8,'cel'=32] {'sta'}, dimensions={0}, use_global_device_ids=true | all-gather | bytes 294912 | tf_op jit(solution)/shard_map/all_gather | solution.py:87
  30.4 0.6 gather_fusion.3
  31.0 1.4 gather_fusion.5
  32.4 0.7 gather_fusion.4
  33.3 2.0 select_bitcast_fusion.2
  35.3 3.9 fusion.88
  39.2 5.2 fusion.82
  44.5 17.5 %while.26 = (s32[]{:T(128)}, f32[16,128,256]{2,1,0:T(8,128)}, s32[]{:T(128)}, s32[64]{0:T(128)S(1)}, s32[]{:T(128)}, /*index=5*/f32[3,128,256]{2,0,1:T(4,128)}, ...) while((s32[]{:T(128)}, f32[16,128,256]{2,1,0:T(8,128)}, ...), condition=%wide.region_1.3_spmd.clone, body=%wide.region_0.0_spmd.clone.sunk | while | flops 79176800 | bytes 21598760 | solution.py:59
  44.5 0.7 compare_and_fusion.5
  45.2 1.6 gather_fusion.2
  47.0 3.3 convolution_bitcast_fusion.2
  50.3 1.6 bitcast_add_fusion.2
  51.9 1.3 copy-done.2
  53.2 0.7 compare_and_fusion.5
  54.0 1.6 gather_fusion.2
  55.7 3.3 convolution_bitcast_fusion.2
  59.0 1.6 bitcast_add_fusion.2
  60.6 1.3 copy-done.2
  62.0 4.2 copy.46
  66.2 0.7 dynamic_slice.37
  66.9 263.1 %reduce-scatter.2.cloned.1.call-done = f32[16,1024]{1,0:T(8,128)} async-done(((f32[16,32768]{1,0:T(8,128)}), f32[16,1024]{1,0:T(8,128)}) %reduce-scatter.2.cloned.1.call-update) | async-done | bytes 65552 | tf_op jit(solution)/shard_map/reduce_scatter | solution.py:120
  330.0 1.5 multiply_convert_fusion
  331.6 77.0 %all-gather.3.cloned.1.call-done = bf16[16,32768]{1,0:T(8,128)(2,1)} async-done(((bf16[16,1024]{1,0:T(8,128)(2,1)}), bf16[16,32768]{1,0:T(8,128)(2,1)}) %all-gather.3.cloned.1.call-update) | async-done | bytes 1048592 | tf_op jit(solution)/shard_map/all_gather | solution.py:123
  408.6 1.3 copy.74
  409.9 1.1 broadcast_in_dim.105.clone
  411.0 15.3 %while.25 = (s32[]{:T(128)}, f32[16,64,256]{2,1,0:T(8,128)}, s32[]{:T(128)}, s32[]{:T(128)}, s32[64]{0:T(128)S(1)}, /*index=5*/f32[3,128,256]{2,0,1:T(4,128)}, f...) while((s32[]{:T(128)}, f32[16,64,256]{2,1,0:T(8,128)}, ...), condition=%wide.region_4.6_spmd, body=%wide.region_3.5_spmd.sunk | while | flops 28384328 | bytes 889271 | solution.py:78
  411.0 0.7 dynamic-slice_bitcast_fusion.8
  411.7 0.7 compare_and_fusion.4
  412.4 1.6 gather_fusion
  414.8 3.1 fusion.161
  417.9 0.8 copy_dynamic-update-slice_fusion.2
  418.7 0.7 dynamic-slice_bitcast_fusion.8
  419.4 0.7 compare_and_fusion.4
  420.1 1.6 gather_fusion
  422.4 3.1 fusion.161
  425.5 0.8 copy_dynamic-update-slice_fusion.2
  426.3 1.7 gather_fusion.6
  428.0 2.6 fusion.135
  430.6 3.9 fusion.85
  434.5 3.6 fusion.110
  438.1 0.9 copy.47
  440.2 109.3 %all-reduce.3.cloned.1.call-done = bf16[16,8192]{1,0:T(8,128)(2,1)} async-done(((bf16[16,8192]{1,0:T(8,128)(2,1)}), bf16[16,8192]{1,0:T(8,128)(2,1)}) %all-reduce.3.cloned.1.call-update) | async-done | bytes 262160
  549.5 1.6 dynamic-slice_convert_fusion
  (72 shorter events, 2.9 us)
Async XLA Ops:
  7.2 28.2 %copy-start = (bf16[1,1,128,32,256]{4,3,2,1,0:T(8,128)(2,1)S(1)}, bf16[1,1,128,32,256]{4,3,2,1,0:T(8,128)(2,1)}, u32[]{:S(2)}) copy-start(bf16[1,1,128,32,256]{4,3,2,1,0:T(8,128)(2,1)} %param.22) | copy-start | bytes 6291460
  7.2 322.9 %reduce-scatter.2.cloned.1.call-start = ((), (), s32[]{:S(2)}) async-start(), calls=%async_computation.1 | async-start | bytes 2162688 | tf_op jit(solution)/shard_map/reduce_scatter | solution.py:120
  30.0 2.4 copy-start.5
  31.0 4.3 copy-start.11
  35.3 3.9 copy-start.8
  47.0 3.3 copy-start.1
  51.9 1.3 copy-start.2
  55.7 3.3 copy-start.1
  60.6 1.3 copy-start.2
  62.0 4.2 copy-start.4
  66.1 265.4 %copy-start.9 = (s32[128]{0:T(128)S(1)}, s32[128]{0:T(128)}, u32[]{:S(2)}) copy-start(s32[128]{0:T(128)} %get-tuple-element.343) | copy-start | bytes 1540
  66.2 342.5 %all-gather.3.cloned.1.call-start = ((), (), s32[]{:S(2)}) async-start(), calls=%async_computation.2 | async-start | bytes 1081344 | tf_op jit(solution)/shard_map/all_gather | solution.py:123
  331.5 218.0 %all-reduce.3.cloned.1.call-start = ((), (), s32[]{:S(2)}) async-start(), calls=%async_computation.3 | async-start | bytes 524288
  426.3 1.7 copy-start.6
  426.3 4.3 copy-start.10
  428.0 2.6 copy-start.3
  430.6 3.9 copy-start.7
  434.5 4.5 copy-start.12
Sparse Core Ops, SparseCore 0:
  66.3 263.7 reduce-scatter.1
  333.5 75.0 all-gather.2
  439.1 110.4 all-reduce.2
where the time goes:
time: 562 us; the launch traced here: 558 us
  waiting for transfers between devices  450 us (80%)
  matrix products  35.2 us (6%)
  local copies, waits for them, and re-layouts  28.1 us (5%)
  blocking collectives  16.1 us (3%)
  between operations  15.2 us (3%)
  other arithmetic  13.1 us (2%)
    reduce_scatter x1, waiting for transfers between devices, body(): lax.psum_scatter(partial_data, 'cel', scatter_dimension=1, tiled=True)  263 us
    unnamed x4, waiting for transfers between devices  109 us
    all_gather x1, waiting for transfers between devices, body(): weighted = lax.all_gather(weighted_share, 'cel', axis=1, tiled=True)  77 us
    all_gather x1, blocking collectives, body(): vectors = lax.all_gather(model_vectors, 'sta', axis=0, tiled=True)  16.1 us
  transfers between devices with their start and end apart: 3, of which 3 were waited for; matrix products, arithmetic and copies ran while one was open for 0% of the time, Pallas kernels for 0%

commit v1 on v0

v1 whole, which is shorter than its diff:
```python
import functools

import jax
import jax.numpy as jnp
from jax import lax
from jax.experimental import pallas as pl
from jax.experimental.pallas import tpu as pltpu
from jax.sharding import PartitionSpec as P

VOLUME = 0.03125
FIELD = (0.17101, 0.46985, -0.86603)
ROOT = (3.0 * VOLUME) ** 0.5

TILE = 256
VECS = 16
GROUP = 8
MIB = 1 << 20
F32 = jnp.float32
BF16 = jnp.bfloat16

SMEM = pl.BlockSpec(memory_space=pltpu.SMEM)
VMEM = pl.BlockSpec(memory_space=pltpu.VMEM)
ANY = pl.BlockSpec(memory_space=pl.ANY)


def split3(x):
    high = x.astype(BF16).astype(F32)
    rest = x - high
    middle = rest.astype(BF16).astype(F32)
    return high, middle, rest - middle


def near_kernel(meta, pairs, stations, cells, out, station_rows, cell_rows):
    step = pl.program_id(0)
    count = meta[0]

    @pl.when(step == 0)
    def _():
        def station_chunk(i, carry):
            at = pl.ds(pl.multiple_of(i * 2048, 2048), 2048)
            x, y, z = (stations[d : d + 1, at] for d in range(3))
            station_rows[0:1, at] = x
            station_rows[1:2, at] = y
            station_rows[2:3, at] = z
            station_rows[3:4, at] = x * x + y * y + z * z
            station_rows[4:5, at] = ROOT * (FIELD[0] * x + FIELD[1] * y + FIELD[2] * z)
            station_rows[5:6, at] = jnp.ones_like(x)
            station_rows[6:8, at] = jnp.zeros((2, 2048), F32)
            return carry

        lax.fori_loop(0, stations.shape[1] // 2048, station_chunk, 0)

        def cell_chunk(i, carry):
            at = pl.ds(pl.multiple_of(i * TILE, TILE), TILE)
            x, y, z = (cells[d : d + 1, at] for d in range(3))
            zero = jnp.zeros_like(x)
            one = jnp.ones_like(x)
            square = x * x + y * y + z * z
            along = -ROOT * (FIELD[0] * x + FIELD[1] * y + FIELD[2] * z)
            lines = lax.broadcasted_iota(jnp.int32, (8, TILE), 0)

            def stack(values):
                total = jnp.zeros((8, TILE), F32)
                for line, value in values:
                    total = jnp.where(lines == line, value, total)
                return total

            wide = stack(((0, -2.0 * x), (1, -2.0 * y), (2, -2.0 * z), (3, one), (5, square)))
            flat = stack(((4, one), (5, along)))
            for position, block in enumerate((wide, flat)):
                h, m, l = split3(block)
                turned = jnp.concatenate((h, h, h, m, m, l), axis=0).T
                cell_rows[i, position * TILE : (position + 1) * TILE, :] = turned.astype(BF16)
            return carry

        lax.fori_loop(0, cells.shape[1] // TILE, cell_chunk, 0)

    @pl.when(step * GROUP < count)
    def _():
        for j in range(GROUP):
            row = pairs[0, step * GROUP + j]
            column = pairs[1, step * GROUP + j]
            at = pl.ds(pl.multiple_of(row * TILE, TILE), TILE)
            h, m, l = split3(station_rows[:, at])
            right = jnp.concatenate((h, m, l, h, m, h), axis=0).astype(BF16)
            both = jnp.dot(cell_rows[column], right, preferred_element_type=F32)
            distance, along = both[:TILE], both[TILE:]
            inverse = lax.rsqrt(distance)
            square = inverse * inverse
            out[j] = ((along * along * square - VOLUME) * (square * inverse)).astype(BF16)


def block_mask():
    lines = lax.broadcasted_iota(jnp.int32, (GROUP * VECS, TILE), 0) // VECS
    lanes = lax.broadcasted_iota(jnp.int32, (GROUP * VECS, TILE), 1) // (TILE // GROUP)
    return lines == lanes


def fetch_blocks(blocks, held, sem, groups):
    def start(g, carry):
        at = pl.ds(g * GROUP, GROUP)
        pltpu.make_async_copy(blocks.at[at], held.at[at], sem.at[g]).start()
        return carry

    lax.fori_loop(0, groups, start, 0)


def await_group(blocks, held, sem, g):
    at = pl.ds(g * GROUP, GROUP)
    pltpu.make_async_copy(blocks.at[at], held.at[at], sem.at[g]).wait()


def contract(a, b, dim):
    return lax.dot_general(a, b, (((1,), (dim,)), ((), ())), preferred_element_type=F32)


def lanes_of(column):
    return pl.ds(pl.multiple_of(column * TILE, TILE), TILE)


def place(meta, row):
    share = row >> 2
    slot = ((share & 3) ^ meta[1]) * 8 + ((share >> 2) ^ meta[2])
    return slot, lanes_of(row & 3)


def forward_kernel(meta, near, mid, *refs):
    parts = refs[:8]
    u_ref, v_ref, blocks = refs[8:11]
    outs = refs[11:15]
    stacked, vectors, total, held, sem = refs[15:]
    groups = meta[0] // GROUP
    fetch_blocks(blocks, held, sem, groups)
    for k in range(8):
        stacked[2 * k : 2 * k + 2, :] = parts[k][...].astype(F32)
    vectors[...] = stacked[...].astype(BF16)
    total[...] = jnp.zeros_like(total)
    mask = block_mask()

    def mid_step(i, carry):
        sums = []
        for q in range(4):
            g = i * 4 + q
            source = jnp.concatenate(
                [vectors[:, lanes_of(mid[1, g * GROUP + j])] for j in range(GROUP)], axis=0
            )
            reduced = contract(source, v_ref[g], 1)
            reduced = jnp.where(mask, reduced, 0.0).astype(BF16)
            sums.append(contract(reduced, u_ref[g], 0))
        for q in range(4):
            for j in range(GROUP):
                slot, lanes = place(meta, mid[0, (i * 4 + q) * GROUP + j])
                total[slot, :, lanes] += sums[q][j * VECS : (j + 1) * VECS]
        return carry

    lax.fori_loop(0, u_ref.shape[0] // 4, mid_step, 0)

    def near_step(g, carry):
        await_group(blocks, held, sem, g)
        sums = [
            contract(vectors[:, lanes_of(near[1, g * GROUP + j])], held[g * GROUP + j], 0)
            for j in range(GROUP)
        ]
        for j in range(GROUP):
            slot, lanes = place(meta, near[0, g * GROUP + j])
            total[slot, :, lanes] += sums[j]
        return carry

    lax.fori_loop(0, groups, near_step, 0)
    for j in range(4):
        outs[j][...] = total[8 * j : 8 * j + 8].astype(outs[j].dtype)


def row_sum_kernel(own, a, b, c, *outs):
    for k in range(8):
        total = own[k] + a[k].astype(F32) + b[k].astype(F32) + c[k].astype(F32)
        outs[k][...] = total.astype(outs[k].dtype)


def weigh_kernel(meta, own, *refs):
    parts = refs[:7]
    weights, predicted, weighted = refs[7:10]
    total = own[...]
    for part in parts:
        total = total + part[...].astype(F32)
    share = weights[pl.ds(pl.multiple_of(meta[3] * 8, 8), 8), :]
    for r in range(8):
        at = slice(r * 128, (r + 1) * 128)
        weighted[:, at] = (total[:, at] * share[r : r + 1, :]).astype(BF16)
    for place_of in range(8):

        @pl.when(meta[4] == place_of)
        def _():
            for k in range(8):
                line = 2 * (k ^ place_of)
                predicted[line : line + 2, :] = total[2 * k : 2 * k + 2]


def join_kernel(*refs):
    for k in range(8):
        refs[8][k] = refs[k][...]


def adjoint_kernel(meta, near, mid, *refs):
    pieces = refs[:4]
    u_ref, v_ref, blocks = refs[4:7]
    outs = refs[7:15]
    data, total, held, sem = refs[15:]
    groups = meta[0] // GROUP
    fetch_blocks(blocks, held, sem, groups)
    for j in range(4):
        data[8 * j : 8 * j + 8] = pieces[j][...]
    total[...] = jnp.zeros_like(total)
    mask = block_mask()

    def station_tile(row):
        slot, lanes = place(meta, row)
        return data[slot, :, lanes]

    def mid_step(i, carry):
        sums = []
        for q in range(4):
            g = i * 4 + q
            source = jnp.concatenate(
                [station_tile(mid[0, g * GROUP + j]) for j in range(GROUP)], axis=0
            )
            pulled = contract(source, u_ref[g], 1)
            pulled = jnp.where(mask, pulled, 0.0).astype(BF16)
            sums.append(contract(pulled, v_ref[g], 0))
        for q in range(4):
            for j in range(GROUP):
                lanes = lanes_of(mid[1, (i * 4 + q) * GROUP + j])
                total[:, lanes] += sums[q][j * VECS : (j + 1) * VECS]
        return carry

    lax.fori_loop(0, u_ref.shape[0] // 4, mid_step, 0)

    def near_step(g, carry):
        await_group(blocks, held, sem, g)
        sums = [
            contract(station_tile(near[0, g * GROUP + j]), held[g * GROUP + j], 1)
            for j in range(GROUP)
        ]
        for j in range(GROUP):
            total[:, lanes_of(near[1, g * GROUP + j])] += sums[j]
        return carry

    lax.fori_loop(0, groups, near_step, 0)
    for k in range(8):
        outs[k][...] = total[2 * k : 2 * k + 2, :].astype(outs[k].dtype)


def params(mib):
    return pltpu.CompilerParams(vmem_limit_bytes=mib * MIB)


def body(
    model_vectors, station_xyz, cell_xyz, weights, near_pairs, near_count, mid_pairs, mid_u, mid_v
):
    sta_index = lax.axis_index("sta")
    cel_index = lax.axis_index("cel")
    slots = near_pairs.shape[2]
    z_index = cel_index // 4
    y_index = cel_index % 4
    own_count = near_count[0, cel_index]
    meta = jnp.stack([own_count, y_index, z_index, cel_index, sta_index]).astype(jnp.int32)
    near = near_pairs[0, 0].T
    mid = mid_pairs[0, 0].T
    u_factor = mid_u.reshape(-1, TILE, TILE)
    v_factor = mid_v.reshape(-1, TILE, TILE)

    def over_sta(x, k):
        return lax.ppermute(x, "sta", [(i, i ^ k) for i in range(8)])

    def over_y(x, j):
        return lax.ppermute(x, "cel", [(i, i ^ j) for i in range(32)])

    def over_z(x, k):
        return lax.ppermute(x, "cel", [(i, i ^ (4 * k)) for i in range(32)])

    vector_parts = [model_vectors] + [over_sta(model_vectors, k) for k in range(1, 8)]

    blocks = pl.pallas_call(
        near_kernel,
        grid_spec=pltpu.PrefetchScalarGridSpec(
            num_scalar_prefetch=2,
            grid=(slots // GROUP,),
            in_specs=[
                pl.BlockSpec(station_xyz.shape, lambda i, meta, pairs: (0, 0)),
                pl.BlockSpec(cell_xyz.shape, lambda i, meta, pairs: (0, 0)),
            ],
            out_specs=pl.BlockSpec(
                (GROUP, TILE, TILE),
                lambda i, meta, pairs: (jnp.minimum(i, meta[0] // GROUP - 1), 0, 0),
            ),
            scratch_shapes=[
                pltpu.VMEM((8, station_xyz.shape[1]), F32),
                pltpu.VMEM((cell_xyz.shape[1] // TILE, 2 * TILE, 48), BF16),
            ],
        ),
        out_shape=jax.ShapeDtypeStruct((slots, TILE, TILE), BF16),
        compiler_params=params(24),
        cost_estimate=pl.CostEstimate(
            flops=slots * 2 * 512 * 48 * 256, bytes_accessed=10 * MIB, transcendentals=slots * 65536
        ),
        name="near_blocks",
    )(meta, near, station_xyz, cell_xyz)

    wide = jax.ShapeDtypeStruct((8, VECS, 1024), BF16)
    shares = pl.pallas_call(
        forward_kernel,
        in_specs=[SMEM] * 3 + [VMEM] * 10 + [ANY],
        out_specs=[VMEM] * 4,
        out_shape=[jax.ShapeDtypeStruct(wide.shape, F32)] + [wide] * 3,
        scratch_shapes=[
            pltpu.VMEM((VECS, 8192), F32),
            pltpu.VMEM((VECS, 8192), BF16),
            pltpu.VMEM((32, VECS, 1024), F32),
            pltpu.VMEM((slots, TILE, TILE), BF16),
            pltpu.SemaphoreType.DMA((slots // GROUP,)),
        ],
        compiler_params=params(32),
        name="forward",
    )(meta, near, mid, *vector_parts, u_factor, v_factor, blocks)

    from_y = [over_y(shares[j], j) for j in range(1, 4)]
    narrow = jax.ShapeDtypeStruct((VECS, 1024), BF16)
    sums = pl.pallas_call(
        row_sum_kernel,
        in_specs=[VMEM] * 4,
        out_specs=[VMEM] * 8,
        out_shape=[jax.ShapeDtypeStruct(narrow.shape, F32)] + [narrow] * 7,
        compiler_params=params(8),
        name="row_sum",
    )(shares[0], *from_y)
    from_z = [over_z(sums[k], k) for k in range(1, 8)]
    predicted, weighted = pl.pallas_call(
        weigh_kernel,
        in_specs=[SMEM] + [VMEM] * 9,
        out_specs=[VMEM] * 2,
        out_shape=[jax.ShapeDtypeStruct(narrow.shape, F32), narrow],
        compiler_params=params(4),
        name="weigh",
    )(meta, sums[0], *from_z, weights.reshape(-1, 128))

    gathered = [weighted] + [over_z(weighted, k) for k in range(1, 8)]
    column = pl.pallas_call(
        join_kernel,
        in_specs=[VMEM] * 8,
        out_specs=VMEM,
        out_shape=wide,
        compiler_params=params(4),
        name="join",
    )(*gathered)
    columns = [column] + [over_y(column, j) for j in range(1, 4)]

    pair = jax.ShapeDtypeStruct((2, 8192), BF16)
    terms = pl.pallas_call(
        adjoint_kernel,
        in_specs=[SMEM] * 3 + [VMEM] * 6 + [ANY],
        out_specs=[VMEM] * 8,
        out_shape=[jax.ShapeDtypeStruct(pair.shape, F32)] + [pair] * 7,
        scratch_shapes=[
            pltpu.VMEM((32, VECS, 1024), BF16),
            pltpu.VMEM((VECS, 8192), F32),
            pltpu.VMEM((slots, TILE, TILE), BF16),
            pltpu.SemaphoreType.DMA((slots // GROUP,)),
        ],
        compiler_params=params(32),
        name="adjoint",
    )(meta, near, mid, *columns, u_factor, v_factor, blocks)
    gradient = terms[0]
    for k in range(1, 8):
        gradient = gradient + over_sta(terms[k], k).astype(F32)
    return (predicted, gradient)


def solution(mesh):
    return jax.shard_map(
        body,
        mesh=mesh,
        in_specs=(
            P("sta", "cel"),
            P(None, "sta"),
            P(None, "cel"),
            P("sta"),
            P("sta", "cel", None, None),
            P("sta", None),
            P("sta", "cel", None, None),
            P("sta", "cel", None, None, None),
            P("sta", "cel", None, None, None),
        ),
        out_specs=(P(None, ("sta", "cel")), P("sta", "cel")),
        check_vma=False,
    )
```

time: 562 us -> 122 us (0.22)
  waiting for transfers between devices: 450 us -> 25.4 us
  starting transfers between devices: 0.12 us -> 72.4 us
  matrix products: 35.2 us -> 0 us
  local copies, waits for them, and re-layouts: 28.1 us -> 3.97 us
  Pallas kernels: 0 us -> 18.4 us
  blocking collectives: 16.1 us -> 0 us
  between operations: 15.2 us -> 0.83 us
  other arithmetic: 13.1 us -> 0.75 us
    reduce_scatter x1 -> x0, waiting for transfers between devices: 263 us -> none  [body(): lax.psum_scatter(partial_data, 'cel', scatter_dimension=1, tiled=True)]
    unnamed x4 -> x0, waiting for transfers between devices: 109 us -> none
    all_gather x1 -> x0, waiting for transfers between devices: 77 us -> none  [body(): weighted = lax.all_gather(weighted_share, 'cel', axis=1, tiled=True)]
    ppermute x0 -> x34, starting transfers between devices: none -> 72.4 us  [the longest x14 34.4 us: over_z(): return lax.ppermute(x, 'cel', [(i, i ^ 4 * k) for i in range(32)])]
    dot_general x11 -> x0, matrix products: 35.2 us -> none  [the longest x2 6.61 us: forward_advance(): jnp.einsum('vbc,bcs->vbs', source, kernel_blocks, preferred_element_type=...]
    ppermute x0 -> x34, waiting for transfers between devices: none -> 25.4 us  [the longest x6 17 us: over_y(): return lax.ppermute(x, 'cel', [(i, i ^ j) for i in range(32)])]
    pallas_call x0 -> x6, Pallas kernels: none -> 18.4 us  [the longest x1 6.21 us: body(): pl.pallas_call(near_kernel, grid_spec=pltpu.PrefetchScalarGridSpec(num_sc...]
    all_gather x1 -> x0, blocking collectives: 16.1 us -> none  [body(): vectors = lax.all_gather(model_vectors, 'sta', axis=0, tiled=True)]
  transfers between devices with their start and end apart: 3 -> 34, of which waited for: 3 -> 11; matrix products, arithmetic and copies ran while one was open for 0% -> 1% of each run, Pallas kernels for 0% -> 5%
where the time goes in v1:
time: 122 us
  starting transfers between devices  72.4 us (59%)
  waiting for transfers between devices  25.4 us (21%)
  Pallas kernels  18.4 us (15%)
  local copies, waits for them, and re-layouts  3.97 us (3%)
    ppermute x14, starting transfers between devices, over_z(): return lax.ppermute(x, 'cel', [(i, i ^ 4 * k) for i in range(32)])  34.4 us
    ppermute x14, starting transfers between devices, over_sta(): return lax.ppermute(x, 'sta', [(i, i ^ k) for i in range(8)])  30.8 us
    ppermute x6, waiting for transfers between devices, over_y(): return lax.ppermute(x, 'cel', [(i, i ^ j) for i in range(32)])  17 us
    ppermute x6, starting transfers between devices, over_y(): return lax.ppermute(x, 'cel', [(i, i ^ j) for i in range(32)])  7.28 us
    ppermute x14, waiting for transfers between devices, over_z(): return lax.ppermute(x, 'cel', [(i, i ^ 4 * k) for i in range(32)])  6.31 us
    pallas_call x1, Pallas kernels, body(): pl.pallas_call(near_kernel, grid_spec=pltpu.PrefetchScalarGridSpec(num_sc...  6.21 us
    pallas_call x1, Pallas kernels, body(): pl.pallas_call(adjoint_kernel, in_specs=[SMEM] * 3 + [VMEM] * 6 + [ANY],...  5.43 us
    pallas_call x1, Pallas kernels, body(): pl.pallas_call(forward_kernel, in_specs=[SMEM] * 3 + [VMEM] * 10 + [ANY],...  5.38 us
  transfers between devices with their start and end apart: 34, of which 11 were waited for; matrix products, arithmetic and copies ran while one was open for 1% of the time, Pallas kernels for 5%

profile of v1, /device:TPU:1, one launch (start us, length us, event | category | flops | bytes accessed | tf_op | source)
XLA Modules:
  0.0 121.8 jit_solution(2494551974296190487)
XLA Ops:
  0.6 3.4 %collective-permute-start.5 = (bf16[2,8192]{1,0:T(2,128)(2,1)}, bf16[2,8192]{1,0:T(2,128)(2,1)S(1)}, u32[]{:S(2)}, u32[]{:S(2)}) collective-permute-start(bf16[2,8192]{1,0:T(2,128)(2,1)} %refs_0_.1), channel_id=1, source_target_pairs={{0,192},{32,224},{64,128},{96,160},{128,64},{160,96},{192,0},{224,... | collective-permute-start | bytes 98312 | tf_op jit(solution)/shard_map/ppermute | solution.py:273
  4.0 1.4 %collective-permute-start.4 = (bf16[2,8192]{1,0:T(2,128)(2,1)}, bf16[2,8192]{1,0:T(2,128)(2,1)S(1)}, u32[]{:S(2)}, u32[]{:S(2)}) collective-permute-start(bf16[2,8192]{1,0:T(2,128)(2,1)} %refs_0_.1), channel_id=1, source_target_pairs={{0,160},{32,128},{64,224},{96,192},{128,32},{160,0},{192,96},{224,... | collective-permute-start | bytes 98312 | tf_op jit(solution)/shard_map/ppermute | solution.py:273
  5.4 2.5 %collective-permute-start.3 = (bf16[2,8192]{1,0:T(2,128)(2,1)}, bf16[2,8192]{1,0:T(2,128)(2,1)S(1)}, u32[]{:S(2)}, u32[]{:S(2)}) collective-permute-start(bf16[2,8192]{1,0:T(2,128)(2,1)} %refs_0_.1), channel_id=1, source_target_pairs={{0,128},{32,160},{64,192},{96,224},{128,0},{160,32},{192,64},{224,... | collective-permute-start | bytes 98312 | tf_op jit(solution)/shard_map/ppermute | solution.py:273
  7.9 1.2 collective-permute-start.1
  9.0 0.6 constant_dynamic-slice_fusion
  9.6 0.7 stack.19.meta
  10.4 1.0 collective-permute-start
  11.3 1.9 %collective-permute-start.6 = (bf16[2,8192]{1,0:T(2,128)(2,1)}, bf16[2,8192]{1,0:T(2,128)(2,1)S(1)}, u32[]{:S(2)}, u32[]{:S(2)}) collective-permute-start(bf16[2,8192]{1,0:T(2,128)(2,1)} %refs_0_.1), channel_id=1, source_target_pairs={{0,224},{32,192},{64,160},{96,128},{128,96},{160,64},{192,32},{224... | collective-permute-start | bytes 98312 | tf_op jit(solution)/shard_map/ppermute | solution.py:273
  13.3 1.0 copy-done.3
  14.3 0.9 copy-done.4
  15.2 0.7 copy-done.7
  15.9 6.2 %near_blocks.1.refs_10_.refs_6_ = bf16[64,256,256]{2,1,0:T(8,128)(2,1)S(1)} custom-call(s32[5]{0:T(128)S(1)} %stack.19.meta, s32[2,64]{1,0:T(2,128)S(1)} %bitcast.19, f32[3,32768]{1,0:T(4,128)S(1)} %copy-done.3, f32[3,8192]{1,0:T(4,128)S(1)} %copy-done.4), custom_call_target="tpu_custom_call" | custom-call | flops 805306368 | bytes 10485760 | tf_op jit(solution)/shard_map/near_blocks/pallas_call | solution.py:283
  22.2 5.4 %forward.1 = (f32[8,16,1024]{2,1,0:T(8,128)S(1)}, bf16[8,16,1024]{2,1,0:T(8,128)(2,1)S(1)}, bf16[8,16,1024]{2,1,0:T(8,128)(2,1)S(1)}, bf16[8,16,1024]{2,1,0:T(8,128)(2,1)S(1)}) custom-call(s32[5]{0:T(128)S(1)} %stack.19.meta, s32[2,64]{1,0:T(2,128)S(1)} %bitcast.20, s32[2,128]{1,0:T(2,128)S(1)} %bitcast.22, bf16[2,8192]{1,0:T(2,128)(2,1)S(1)} %copy-done.6, ...), custom_call_target="tpu_custom_call" | custom-call | tf_op jit(solution)/shard_map/forward/pallas_call | solution.py:310
  27.6 0.1 collective-permute-start.7
  27.7 3.5 %collective-permute-start.8 = (bf16[8,16,1024]{2,1,0:T(8,128)(2,1)S(1)}, bf16[8,16,1024]{2,1,0:T(8,128)(2,1)S(1)}, u32[]{:S(2)}, u32[]{:S(2)}) collective-permute-start(bf16[8,16,1024]{2,1,0:T(8,128)(2,1)S(1)} %get-tuple-element.26), channel_id=1, source_target_pairs={{0,2},{1,3},{2,0},{3,1},{4,6},{5,7},{6,4},{7,5},{8,10},{9,11},{10,... | collective-permute-start | bytes 786440 | tf_op jit(solution)/shard_map/ppermute | solution.py:276
  31.2 0.4 collective-permute-start.9
  31.6 1.4 %collective-permute-done.7.a = bf16[8,16,1024]{2,1,0:T(8,128)(2,1)S(1)} collective-permute-done((bf16[8,16,1024]{2,1,0:T(8,128)(2,1)S(1)}, bf16[8,16,1024]{2,1,0:T(8,128)(2,1)S(1)}, u32[]{:S(2)}, u32[]{:S(2)}) %collective-permute-start.7) | collective-permute-done | bytes 262176 | tf_op jit(solution)/shard_map/ppermute | solution.py:276
  32.9 9.0 %collective-permute-done.8.b = bf16[8,16,1024]{2,1,0:T(8,128)(2,1)S(1)} collective-permute-done((bf16[8,16,1024]{2,1,0:T(8,128)(2,1)S(1)}, bf16[8,16,1024]{2,1,0:T(8,128)(2,1)S(1)}, u32[]{:S(2)}, u32[]{:S(2)}) %collective-permute-start.8) | collective-permute-done | bytes 262176 | tf_op jit(solution)/shard_map/ppermute | solution.py:276
  42.0 0.1 row_sum.1
  42.1 9.0 %collective-permute-start.10 = (bf16[16,1024]{1,0:T(8,128)(2,1)S(1)}, bf16[16,1024]{1,0:T(8,128)(2,1)S(1)}, u32[]{:S(2)}, u32[]{:S(2)}) collective-permute-start(bf16[16,1024]{1,0:T(8,128)(2,1)S(1)} %get-tuple-element.29), channel_id=1, source_target_pairs={{0,4},{1,5},{2,6},{3,7},{4,0},{5,1},{6,2},{7,3},{8,12},{9,13},{10,... | collective-permute-start | bytes 98312 | tf_op jit(solution)/shard_map/ppermute | solution.py:279
  51.1 1.4 %collective-permute-start.11 = (bf16[16,1024]{1,0:T(8,128)(2,1)S(1)}, bf16[16,1024]{1,0:T(8,128)(2,1)S(1)}, u32[]{:S(2)}, u32[]{:S(2)}) collective-permute-start(bf16[16,1024]{1,0:T(8,128)(2,1)S(1)} %get-tuple-element.30), channel_id=1, source_target_pairs={{0,8},{1,9},{2,10},{3,11},{4,12},{5,13},{6,14},{7,15},{8,0},{9,1},... | collective-permute-start | bytes 98312 | tf_op jit(solution)/shard_map/ppermute | solution.py:279
  52.6 1.1 collective-permute-start.12
  53.7 6.1 %collective-permute-start.13 = (bf16[16,1024]{1,0:T(8,128)(2,1)S(1)}, bf16[16,1024]{1,0:T(8,128)(2,1)S(1)}, u32[]{:S(2)}, u32[]{:S(2)}) collective-permute-start(bf16[16,1024]{1,0:T(8,128)(2,1)S(1)} %get-tuple-element.32), channel_id=1, source_target_pairs={{0,16},{1,17},{2,18},{3,19},{4,20},{5,21},{6,22},{7,23},{8,24},{9,... | collective-permute-start | bytes 98312 | tf_op jit(solution)/shard_map/ppermute | solution.py:279
  59.8 5.1 %collective-permute-start.15 = (bf16[16,1024]{1,0:T(8,128)(2,1)S(1)}, bf16[16,1024]{1,0:T(8,128)(2,1)S(1)}, u32[]{:S(2)}, u32[]{:S(2)}) collective-permute-start(bf16[16,1024]{1,0:T(8,128)(2,1)S(1)} %get-tuple-element.34), channel_id=1, source_target_pairs={{0,24},{1,25},{2,26},{3,27},{4,28},{5,29},{6,30},{7,31},{8,16},{9,... | collective-permute-start | bytes 98312 | tf_op jit(solution)/shard_map/ppermute | solution.py:279
  64.9 0.6 collective-permute-done.14.refs_4_
  65.5 0.6 collective-permute-done.15.refs_5_
  66.2 3.3 %collective-permute-done.16.refs_6_ = bf16[16,1024]{1,0:T(8,128)(2,1)S(1)} collective-permute-done((bf16[16,1024]{1,0:T(8,128)(2,1)S(1)}, bf16[16,1024]{1,0:T(8,128)(2,1)S(1)}, u32[]{:S(2)}, u32[]{:S(2)}) %collective-permute-start.16) | collective-permute-done | bytes 32800 | tf_op jit(solution)/shard_map/ppermute | solution.py:279
  69.5 1.3 %weigh.1 = (f32[16,1024]{1,0:T(8,128)}, bf16[16,1024]{1,0:T(8,128)(2,1)S(1)}) custom-call(s32[5]{0:T(128)S(1)} %stack.19.meta, f32[16,1024]{1,0:T(8,128)S(1)} %get-tuple-element.28.own, bf16[16,1024]{1,0:T(8,128)(2,1)S(1)} %collective-permute-done.10.refs_0_, bf16[16,1024]{1,0:T(8,128)(2,1)S(1)} %collective-permute-done.11.refs_1_, ...), custom_call_target="tpu_custom_call" | custom-call | tf_op jit(solution)/shard_map/weigh/pallas_call | solution.py:337
  70.8 0.4 collective-permute-start.23
  71.2 3.3 %collective-permute-start.22 = (bf16[16,1024]{1,0:T(8,128)(2,1)S(1)}, bf16[16,1024]{1,0:T(8,128)(2,1)S(1)}, u32[]{:S(2)}, u32[]{:S(2)}) collective-permute-start(bf16[16,1024]{1,0:T(8,128)(2,1)S(1)} %get-tuple-element.37.refs_0_), channel_id=1, source_target_pairs={{0,24},{1,25},{2,26},{3,27},{4,28},{5,29},{6,30},{7,31},{8,16},{9,... | collective-permute-start | bytes 98312 | tf_op jit(solution)/shard_map/ppermute | solution.py:279
  74.5 4.3 %collective-permute-start.20 = (bf16[16,1024]{1,0:T(8,128)(2,1)S(1)}, bf16[16,1024]{1,0:T(8,128)(2,1)S(1)}, u32[]{:S(2)}, u32[]{:S(2)}) collective-permute-start(bf16[16,1024]{1,0:T(8,128)(2,1)S(1)} %get-tuple-element.37.refs_0_), channel_id=1, source_target_pairs={{0,16},{1,17},{2,18},{3,19},{4,20},{5,21},{6,22},{7,23},{8,24},{9,... | collective-permute-start | bytes 98312 | tf_op jit(solution)/shard_map/ppermute | solution.py:279
  78.8 2.5 %collective-permute-start.18 = (bf16[16,1024]{1,0:T(8,128)(2,1)S(1)}, bf16[16,1024]{1,0:T(8,128)(2,1)S(1)}, u32[]{:S(2)}, u32[]{:S(2)}) collective-permute-start(bf16[16,1024]{1,0:T(8,128)(2,1)S(1)} %get-tuple-element.37.refs_0_), channel_id=1, source_target_pairs={{0,8},{1,9},{2,10},{3,11},{4,12},{5,13},{6,14},{7,15},{8,0},{9,1},... | collective-permute-start | bytes 98312 | tf_op jit(solution)/shard_map/ppermute | solution.py:279
  81.3 1.1 collective-permute-start.17
  82.4 1.2 %collective-permute-done.19.refs_3_ = bf16[16,1024]{1,0:T(8,128)(2,1)S(1)} collective-permute-done((bf16[16,1024]{1,0:T(8,128)(2,1)S(1)}, bf16[16,1024]{1,0:T(8,128)(2,1)S(1)}, u32[]{:S(2)}, u32[]{:S(2)}) %collective-permute-start.19) | collective-permute-done | bytes 32800 | tf_op jit(solution)/shard_map/ppermute | solution.py:279
  83.6 0.5 collective-permute-done.18.refs_2_
  84.1 1.4 %collective-permute-start.26 = (bf16[8,16,1024]{2,1,0:T(8,128)(2,1)S(1)}, bf16[8,16,1024]{2,1,0:T(8,128)(2,1)S(1)}, u32[]{:S(2)}, u32[]{:S(2)}) collective-permute-start(bf16[8,16,1024]{2,1,0:T(8,128)(2,1)S(1)} %join.1.refs_0_), channel_id=1, source_target_pairs={{0,3},{1,2},{2,1},{3,0},{4,7},{5,6},{6,5},{7,4},{8,11},{9,10},{10,... | collective-permute-start | bytes 786440 | tf_op jit(solution)/shard_map/ppermute | solution.py:276
  85.5 0.9 collective-permute-start.25
  86.4 1.0 collective-permute-start.24
  87.4 6.0 %collective-permute-done.26.refs_3_ = bf16[8,16,1024]{2,1,0:T(8,128)(2,1)S(1)} collective-permute-done((bf16[8,16,1024]{2,1,0:T(8,128)(2,1)S(1)}, bf16[8,16,1024]{2,1,0:T(8,128)(2,1)S(1)}, u32[]{:S(2)}, u32[]{:S(2)}) %collective-permute-start.26) | collective-permute-done | bytes 262176 | tf_op jit(solution)/shard_map/ppermute | solution.py:276
  93.4 0.6 collective-permute-done.24.refs_1_
  94.1 5.4 %adjoint.1 = (f32[2,8192]{1,0:T(2,128)S(1)}, bf16[2,8192]{1,0:T(2,128)(2,1)S(1)}, bf16[2,8192]{1,0:T(2,128)(2,1)S(1)}, bf16[2,8192]{1,0:T(2,128)(2,1)S(1)}, bf16...) custom-call(s32[5]{0:T(128)S(1)} %stack.19.meta, ...), custom_call_target="tpu_custom_call" | custom-call | tf_op jit(solution)/shard_map/adjoint/pallas_call | solution.py:358
  99.5 11.5 %collective-permute-start.27 = (bf16[2,8192]{1,0:T(2,128)(2,1)S(1)}, bf16[2,8192]{1,0:T(2,128)(2,1)S(1)}, u32[]{:S(2)}, u32[]{:S(2)}) collective-permute-start(bf16[2,8192]{1,0:T(2,128)(2,1)S(1)} %get-tuple-element.39), channel_id=1, source_target_pairs={{0,32},{32,0},{64,96},{96,64},{128,160},{160,128},{192,224},{224,1... | collective-permute-start | bytes 98312 | tf_op jit(solution)/shard_map/ppermute | solution.py:273
  111.0 1.7 %collective-permute-start.29 = (bf16[2,8192]{1,0:T(2,128)(2,1)S(1)}, bf16[2,8192]{1,0:T(2,128)(2,1)S(1)}, u32[]{:S(2)}, u32[]{:S(2)}) collective-permute-start(bf16[2,8192]{1,0:T(2,128)(2,1)S(1)} %get-tuple-element.41), channel_id=1, source_target_pairs={{0,96},{32,64},{64,32},{96,0},{128,224},{160,192},{192,160},{224,1... | collective-permute-start | bytes 98312 | tf_op jit(solution)/shard_map/ppermute | solution.py:273
  112.8 3.3 %collective-permute-start.31 = (bf16[2,8192]{1,0:T(2,128)(2,1)S(1)}, bf16[2,8192]{1,0:T(2,128)(2,1)S(1)}, u32[]{:S(2)}, u32[]{:S(2)}) collective-permute-start(bf16[2,8192]{1,0:T(2,128)(2,1)S(1)} %get-tuple-element.43), channel_id=1, source_target_pairs={{0,160},{32,128},{64,224},{96,192},{128,32},{160,0},{192,96},{224,... | collective-permute-start | bytes 98312 | tf_op jit(solution)/shard_map/ppermute | solution.py:273
  116.1 2.9 %collective-permute-start.33 = (bf16[2,8192]{1,0:T(2,128)(2,1)S(1)}, bf16[2,8192]{1,0:T(2,128)(2,1)S(1)}, u32[]{:S(2)}, u32[]{:S(2)}) collective-permute-start(bf16[2,8192]{1,0:T(2,128)(2,1)S(1)} %get-tuple-element.45), channel_id=1, source_target_pairs={{0,224},{32,192},{64,160},{96,128},{128,96},{160,64},{192,32},{224... | collective-permute-start | bytes 98312 | tf_op jit(solution)/shard_map/ppermute | solution.py:273
  119.0 1.1 collective-permute-done.32
  120.0 1.1 collective-permute-done.33
  121.1 0.8 convert_add_fusion
  (49 shorter events, 0.2 us)
Async XLA Ops:
  0.6 8.4 %copy-start = (s32[1,32]{1,0:T(1,128)S(1)}, s32[1,32]{1,0:T(1,128)}, u32[]{:S(2)}) copy-start(s32[1,32]{1,0:T(1,128)} %param.14) | copy-start | bytes 388
  0.6 9.7 %collective-permute-start.5 = (bf16[2,8192]{1,0:T(2,128)(2,1)}, bf16[2,8192]{1,0:T(2,128)(2,1)S(1)}, u32[]{:S(2)}, u32[]{:S(2)}) collective-permute-start(bf16[2,8192]{1,0:T(2,128)(2,1)} %refs_0_.1), channel_id=1, source_target_pairs={{0,192},{32,224},{64,128},{96,160},{128,64},{160,96},{192,0},{224,... | collective-permute-start | bytes 98312 | tf_op jit(solution)/shard_map/ppermute | solution.py:273
  4.0 7.3 %collective-permute-start.4 = (bf16[2,8192]{1,0:T(2,128)(2,1)}, bf16[2,8192]{1,0:T(2,128)(2,1)S(1)}, u32[]{:S(2)}, u32[]{:S(2)}) collective-permute-start(bf16[2,8192]{1,0:T(2,128)(2,1)} %refs_0_.1), channel_id=1, source_target_pairs={{0,160},{32,128},{64,224},{96,192},{128,32},{160,0},{192,96},{224,... | collective-permute-start | bytes 98312 | tf_op jit(solution)/shard_map/ppermute | solution.py:273
  5.4 16.7 %collective-permute-start.3 = (bf16[2,8192]{1,0:T(2,128)(2,1)}, bf16[2,8192]{1,0:T(2,128)(2,1)S(1)}, u32[]{:S(2)}, u32[]{:S(2)}) collective-permute-start(bf16[2,8192]{1,0:T(2,128)(2,1)} %refs_0_.1), channel_id=1, source_target_pairs={{0,128},{32,160},{64,192},{96,224},{128,0},{160,32},{192,64},{224,... | collective-permute-start | bytes 98312 | tf_op jit(solution)/shard_map/ppermute | solution.py:273
  7.9 14.3 %collective-permute-start.2 = (bf16[2,8192]{1,0:T(2,128)(2,1)}, bf16[2,8192]{1,0:T(2,128)(2,1)S(1)}, u32[]{:S(2)}, u32[]{:S(2)}) collective-permute-start(bf16[2,8192]{1,0:T(2,128)(2,1)} %refs_0_.1), channel_id=1, source_target_pairs={{0,96},{32,64},{64,32},{96,0},{128,224},{160,192},{192,160},{224,1... | collective-permute-start | bytes 98312 | tf_op jit(solution)/shard_map/ppermute | solution.py:273
  7.9 14.3 %collective-permute-start.1 = (bf16[2,8192]{1,0:T(2,128)(2,1)}, bf16[2,8192]{1,0:T(2,128)(2,1)S(1)}, u32[]{:S(2)}, u32[]{:S(2)}) collective-permute-start(bf16[2,8192]{1,0:T(2,128)(2,1)} %refs_0_.1), channel_id=1, source_target_pairs={{0,64},{32,96},{64,0},{96,32},{128,192},{160,224},{192,128},{224,1... | collective-permute-start | bytes 98312 | tf_op jit(solution)/shard_map/ppermute | solution.py:273
  10.4 11.8 %collective-permute-start = (bf16[2,8192]{1,0:T(2,128)(2,1)}, bf16[2,8192]{1,0:T(2,128)(2,1)S(1)}, u32[]{:S(2)}, u32[]{:S(2)}) collective-permute-start(bf16[2,8192]{1,0:T(2,128)(2,1)} %refs_0_.1), channel_id=1, source_target_pairs={{0,32},{32,0},{64,96},{96,64},{128,160},{160,128},{192,224},{224,1... | collective-permute-start | bytes 98312 | tf_op jit(solution)/shard_map/ppermute | solution.py:273
  11.3 10.8 %collective-permute-start.6 = (bf16[2,8192]{1,0:T(2,128)(2,1)}, bf16[2,8192]{1,0:T(2,128)(2,1)S(1)}, u32[]{:S(2)}, u32[]{:S(2)}) collective-permute-start(bf16[2,8192]{1,0:T(2,128)(2,1)} %refs_0_.1), channel_id=1, source_target_pairs={{0,224},{32,192},{64,160},{96,128},{128,96},{160,64},{192,32},{224... | collective-permute-start | bytes 98312 | tf_op jit(solution)/shard_map/ppermute | solution.py:273
  13.3 1.0 copy-start.3
  14.3 0.9 copy-start.4
  15.2 0.7 copy-start.7
  15.9 6.3 %copy-start.1 = (bf16[1,1,128,32,256]{4,3,2,1,0:T(8,128)(2,1)S(1)}, bf16[1,1,128,32,256]{4,3,2,1,0:T(8,128)(2,1)}, u32[]{:S(2)}) copy-start(bf16[1,1,128,32,256]{4,3,2,1,0:T(8,128)(2,1)} %param.16) | copy-start | bytes 6291460
  15.9 6.3 %copy-start.2 = (bf16[1,1,128,32,256]{4,3,2,1,0:T(8,128)(2,1)S(1)}, bf16[1,1,128,32,256]{4,3,2,1,0:T(8,128)(2,1)}, u32[]{:S(2)}) copy-start(bf16[1,1,128,32,256]{4,3,2,1,0:T(8,128)(2,1)} %param.17) | copy-start | bytes 6291460
  15.9 6.3 %copy-start.6 = (bf16[2,8192]{1,0:T(2,128)(2,1)S(1)}, bf16[2,8192]{1,0:T(2,128)(2,1)}, u32[]{:S(2)}) copy-start(bf16[2,8192]{1,0:T(2,128)(2,1)} %refs_0_.1) | copy-start | bytes 98308
  15.9 6.3 %copy-start.8 = (s32[1,1,64,2]{2,3,1,0:T(2,128)S(1)}, s32[1,1,64,2]{2,3,1,0:T(2,128)}, u32[]{:S(2)}) copy-start(s32[1,1,64,2]{2,3,1,0:T(2,128)} %param.13) | copy-start | bytes 1540
  15.9 6.3 %copy-start.9 = (s32[1,1,128,2]{2,3,1,0:T(2,128)S(1)}, s32[1,1,128,2]{2,3,1,0:T(2,128)}, u32[]{:S(2)}) copy-start(s32[1,1,128,2]{2,3,1,0:T(2,128)} %param.15) | copy-start | bytes 3076
  22.2 47.2 %copy-start.5 = (f32[32768]{0:T(1024)S(1)}, f32[32768]{0:T(1024)}, u32[]{:S(2)}) copy-start(f32[32768]{0:T(1024)} %param.12) | copy-start | bytes 393220
  27.6 5.3 %collective-permute-start.7 = (bf16[8,16,1024]{2,1,0:T(8,128)(2,1)S(1)}, bf16[8,16,1024]{2,1,0:T(8,128)(2,1)S(1)}, u32[]{:S(2)}, u32[]{:S(2)}) collective-permute-start(bf16[8,16,1024]{2,1,0:T(8,128)(2,1)S(1)} %get-tuple-element.25), channel_id=1, source_target_pairs={{0,1},{1,0},{2,3},{3,2},{4,5},{5,4},{6,7},{7,6},{8,9},{9,8},{10,11... | collective-permute-start | bytes 786440 | tf_op jit(solution)/shard_map/ppermute | solution.py:276
  27.7 14.2 %collective-permute-start.8 = (bf16[8,16,1024]{2,1,0:T(8,128)(2,1)S(1)}, bf16[8,16,1024]{2,1,0:T(8,128)(2,1)S(1)}, u32[]{:S(2)}, u32[]{:S(2)}) collective-permute-start(bf16[8,16,1024]{2,1,0:T(8,128)(2,1)S(1)} %get-tuple-element.26), channel_id=1, source_target_pairs={{0,2},{1,3},{2,0},{3,1},{4,6},{5,7},{6,4},{7,5},{8,10},{9,11},{10,... | collective-permute-start | bytes 786440 | tf_op jit(solution)/shard_map/ppermute | solution.py:276
  31.2 10.8 %collective-permute-start.9 = (bf16[8,16,1024]{2,1,0:T(8,128)(2,1)S(1)}, bf16[8,16,1024]{2,1,0:T(8,128)(2,1)S(1)}, u32[]{:S(2)}, u32[]{:S(2)}) collective-permute-start(bf16[8,16,1024]{2,1,0:T(8,128)(2,1)S(1)} %get-tuple-element.27), channel_id=1, source_target_pairs={{0,3},{1,2},{2,1},{3,0},{4,7},{5,6},{6,5},{7,4},{8,11},{9,10},{10,... | collective-permute-start | bytes 786440 | tf_op jit(solution)/shard_map/ppermute | solution.py:276
  42.1 17.7 %collective-permute-start.10 = (bf16[16,1024]{1,0:T(8,128)(2,1)S(1)}, bf16[16,1024]{1,0:T(8,128)(2,1)S(1)}, u32[]{:S(2)}, u32[]{:S(2)}) collective-permute-start(bf16[16,1024]{1,0:T(8,128)(2,1)S(1)} %get-tuple-element.29), channel_id=1, source_target_pairs={{0,4},{1,5},{2,6},{3,7},{4,0},{5,1},{6,2},{7,3},{8,12},{9,13},{10,... | collective-permute-start | bytes 98312 | tf_op jit(solution)/shard_map/ppermute | solution.py:279
  51.1 13.8 %collective-permute-start.11 = (bf16[16,1024]{1,0:T(8,128)(2,1)S(1)}, bf16[16,1024]{1,0:T(8,128)(2,1)S(1)}, u32[]{:S(2)}, u32[]{:S(2)}) collective-permute-start(bf16[16,1024]{1,0:T(8,128)(2,1)S(1)} %get-tuple-element.30), channel_id=1, source_target_pairs={{0,8},{1,9},{2,10},{3,11},{4,12},{5,13},{6,14},{7,15},{8,0},{9,1},... | collective-permute-start | bytes 98312 | tf_op jit(solution)/shard_map/ppermute | solution.py:279
  52.6 12.3 %collective-permute-start.12 = (bf16[16,1024]{1,0:T(8,128)(2,1)S(1)}, bf16[16,1024]{1,0:T(8,128)(2,1)S(1)}, u32[]{:S(2)}, u32[]{:S(2)}) collective-permute-start(bf16[16,1024]{1,0:T(8,128)(2,1)S(1)} %get-tuple-element.31), channel_id=1, source_target_pairs={{0,12},{1,13},{2,14},{3,15},{4,8},{5,9},{6,10},{7,11},{8,4},{9,5},... | collective-permute-start | bytes 98312 | tf_op jit(solution)/shard_map/ppermute | solution.py:279
  53.7 11.2 %collective-permute-start.13 = (bf16[16,1024]{1,0:T(8,128)(2,1)S(1)}, bf16[16,1024]{1,0:T(8,128)(2,1)S(1)}, u32[]{:S(2)}, u32[]{:S(2)}) collective-permute-start(bf16[16,1024]{1,0:T(8,128)(2,1)S(1)} %get-tuple-element.32), channel_id=1, source_target_pairs={{0,16},{1,17},{2,18},{3,19},{4,20},{5,21},{6,22},{7,23},{8,24},{9,... | collective-permute-start | bytes 98312 | tf_op jit(solution)/shard_map/ppermute | solution.py:279
  59.8 5.8 %collective-permute-start.14 = (bf16[16,1024]{1,0:T(8,128)(2,1)S(1)}, bf16[16,1024]{1,0:T(8,128)(2,1)S(1)}, u32[]{:S(2)}, u32[]{:S(2)}) collective-permute-start(bf16[16,1024]{1,0:T(8,128)(2,1)S(1)} %get-tuple-element.33), channel_id=1, source_target_pairs={{0,20},{1,21},{2,22},{3,23},{4,16},{5,17},{6,18},{7,19},{8,28},{9,... | collective-permute-start | bytes 98312 | tf_op jit(solution)/shard_map/ppermute | solution.py:279
  59.8 6.4 %collective-permute-start.15 = (bf16[16,1024]{1,0:T(8,128)(2,1)S(1)}, bf16[16,1024]{1,0:T(8,128)(2,1)S(1)}, u32[]{:S(2)}, u32[]{:S(2)}) collective-permute-start(bf16[16,1024]{1,0:T(8,128)(2,1)S(1)} %get-tuple-element.34), channel_id=1, source_target_pairs={{0,24},{1,25},{2,26},{3,27},{4,28},{5,29},{6,30},{7,31},{8,16},{9,... | collective-permute-start | bytes 98312 | tf_op jit(solution)/shard_map/ppermute | solution.py:279
  64.9 4.6 %collective-permute-start.16 = (bf16[16,1024]{1,0:T(8,128)(2,1)S(1)}, bf16[16,1024]{1,0:T(8,128)(2,1)S(1)}, u32[]{:S(2)}, u32[]{:S(2)}) collective-permute-start(bf16[16,1024]{1,0:T(8,128)(2,1)S(1)} %get-tuple-element.35), channel_id=1, source_target_pairs={{0,28},{1,29},{2,30},{3,31},{4,24},{5,25},{6,26},{7,27},{8,20},{9,... | collective-permute-start | bytes 98312 | tf_op jit(solution)/shard_map/ppermute | solution.py:279
  70.8 8.1 %collective-permute-start.23 = (bf16[16,1024]{1,0:T(8,128)(2,1)S(1)}, bf16[16,1024]{1,0:T(8,128)(2,1)S(1)}, u32[]{:S(2)}, u32[]{:S(2)}) collective-permute-start(bf16[16,1024]{1,0:T(8,128)(2,1)S(1)} %get-tuple-element.37.refs_0_), channel_id=1, source_target_pairs={{0,28},{1,29},{2,30},{3,31},{4,24},{5,25},{6,26},{7,27},{8,20},{9,... | collective-permute-start | bytes 98312 | tf_op jit(solution)/shard_map/ppermute | solution.py:279
  71.2 10.1 %collective-permute-start.22 = (bf16[16,1024]{1,0:T(8,128)(2,1)S(1)}, bf16[16,1024]{1,0:T(8,128)(2,1)S(1)}, u32[]{:S(2)}, u32[]{:S(2)}) collective-permute-start(bf16[16,1024]{1,0:T(8,128)(2,1)S(1)} %get-tuple-element.37.refs_0_), channel_id=1, source_target_pairs={{0,24},{1,25},{2,26},{3,27},{4,28},{5,29},{6,30},{7,31},{8,16},{9,... | collective-permute-start | bytes 98312 | tf_op jit(solution)/shard_map/ppermute | solution.py:279
  74.4 7.9 %collective-permute-start.21 = (bf16[16,1024]{1,0:T(8,128)(2,1)S(1)}, bf16[16,1024]{1,0:T(8,128)(2,1)S(1)}, u32[]{:S(2)}, u32[]{:S(2)}) collective-permute-start(bf16[16,1024]{1,0:T(8,128)(2,1)S(1)} %get-tuple-element.37.refs_0_), channel_id=1, source_target_pairs={{0,20},{1,21},{2,22},{3,23},{4,16},{5,17},{6,18},{7,19},{8,28},{9,... | collective-permute-start | bytes 98312 | tf_op jit(solution)/shard_map/ppermute | solution.py:279
  74.5 7.9 %collective-permute-start.20 = (bf16[16,1024]{1,0:T(8,128)(2,1)S(1)}, bf16[16,1024]{1,0:T(8,128)(2,1)S(1)}, u32[]{:S(2)}, u32[]{:S(2)}) collective-permute-start(bf16[16,1024]{1,0:T(8,128)(2,1)S(1)} %get-tuple-element.37.refs_0_), channel_id=1, source_target_pairs={{0,16},{1,17},{2,18},{3,19},{4,20},{5,21},{6,22},{7,23},{8,24},{9,... | collective-permute-start | bytes 98312 | tf_op jit(solution)/shard_map/ppermute | solution.py:279
  78.8 4.8 %collective-permute-start.19 = (bf16[16,1024]{1,0:T(8,128)(2,1)S(1)}, bf16[16,1024]{1,0:T(8,128)(2,1)S(1)}, u32[]{:S(2)}, u32[]{:S(2)}) collective-permute-start(bf16[16,1024]{1,0:T(8,128)(2,1)S(1)} %get-tuple-element.37.refs_0_), channel_id=1, source_target_pairs={{0,12},{1,13},{2,14},{3,15},{4,8},{5,9},{6,10},{7,11},{8,4},{9,5},... | collective-permute-start | bytes 98312 | tf_op jit(solution)/shard_map/ppermute | solution.py:279
  78.8 5.3 %collective-permute-start.18 = (bf16[16,1024]{1,0:T(8,128)(2,1)S(1)}, bf16[16,1024]{1,0:T(8,128)(2,1)S(1)}, u32[]{:S(2)}, u32[]{:S(2)}) collective-permute-start(bf16[16,1024]{1,0:T(8,128)(2,1)S(1)} %get-tuple-element.37.refs_0_), channel_id=1, source_target_pairs={{0,8},{1,9},{2,10},{3,11},{4,12},{5,13},{6,14},{7,15},{8,0},{9,1},... | collective-permute-start | bytes 98312 | tf_op jit(solution)/shard_map/ppermute | solution.py:279
  81.3 2.8 %collective-permute-start.17 = (bf16[16,1024]{1,0:T(8,128)(2,1)S(1)}, bf16[16,1024]{1,0:T(8,128)(2,1)S(1)}, u32[]{:S(2)}, u32[]{:S(2)}) collective-permute-start(bf16[16,1024]{1,0:T(8,128)(2,1)S(1)} %get-tuple-element.37.refs_0_), channel_id=1, source_target_pairs={{0,4},{1,5},{2,6},{3,7},{4,0},{5,1},{6,2},{7,3},{8,12},{9,13},{10,... | collective-permute-start | bytes 98312 | tf_op jit(solution)/shard_map/ppermute | solution.py:279
  84.1 9.3 %collective-permute-start.26 = (bf16[8,16,1024]{2,1,0:T(8,128)(2,1)S(1)}, bf16[8,16,1024]{2,1,0:T(8,128)(2,1)S(1)}, u32[]{:S(2)}, u32[]{:S(2)}) collective-permute-start(bf16[8,16,1024]{2,1,0:T(8,128)(2,1)S(1)} %join.1.refs_0_), channel_id=1, source_target_pairs={{0,3},{1,2},{2,1},{3,0},{4,7},{5,6},{6,5},{7,4},{8,11},{9,10},{10,... | collective-permute-start | bytes 786440 | tf_op jit(solution)/shard_map/ppermute | solution.py:276
  85.5 7.9 %collective-permute-start.25 = (bf16[8,16,1024]{2,1,0:T(8,128)(2,1)S(1)}, bf16[8,16,1024]{2,1,0:T(8,128)(2,1)S(1)}, u32[]{:S(2)}, u32[]{:S(2)}) collective-permute-start(bf16[8,16,1024]{2,1,0:T(8,128)(2,1)S(1)} %join.1.refs_0_), channel_id=1, source_target_pairs={{0,2},{1,3},{2,0},{3,1},{4,6},{5,7},{6,4},{7,5},{8,10},{9,11},{10,... | collective-permute-start | bytes 786440 | tf_op jit(solution)/shard_map/ppermute | solution.py:276
  86.4 7.6 %collective-permute-start.24 = (bf16[8,16,1024]{2,1,0:T(8,128)(2,1)S(1)}, bf16[8,16,1024]{2,1,0:T(8,128)(2,1)S(1)}, u32[]{:S(2)}, u32[]{:S(2)}) collective-permute-start(bf16[8,16,1024]{2,1,0:T(8,128)(2,1)S(1)} %join.1.refs_0_), channel_id=1, source_target_pairs={{0,1},{1,0},{2,3},{3,2},{4,5},{5,4},{6,7},{7,6},{8,9},{9,8},{10,11... | collective-permute-start | bytes 786440 | tf_op jit(solution)/shard_map/ppermute | solution.py:276
  99.5 16.6 %collective-permute-start.27 = (bf16[2,8192]{1,0:T(2,128)(2,1)S(1)}, bf16[2,8192]{1,0:T(2,128)(2,1)S(1)}, u32[]{:S(2)}, u32[]{:S(2)}) collective-permute-start(bf16[2,8192]{1,0:T(2,128)(2,1)S(1)} %get-tuple-element.39), channel_id=1, source_target_pairs={{0,32},{32,0},{64,96},{96,64},{128,160},{160,128},{192,224},{224,1... | collective-permute-start | bytes 98312 | tf_op jit(solution)/shard_map/ppermute | solution.py:273
  111.0 5.0 %collective-permute-start.28 = (bf16[2,8192]{1,0:T(2,128)(2,1)S(1)}, bf16[2,8192]{1,0:T(2,128)(2,1)S(1)}, u32[]{:S(2)}, u32[]{:S(2)}) collective-permute-start(bf16[2,8192]{1,0:T(2,128)(2,1)S(1)} %get-tuple-element.40), channel_id=1, source_target_pairs={{0,64},{32,96},{64,0},{96,32},{128,192},{160,224},{192,128},{224,1... | collective-permute-start | bytes 98312 | tf_op jit(solution)/shard_map/ppermute | solution.py:273
  111.0 7.9 %collective-permute-start.29 = (bf16[2,8192]{1,0:T(2,128)(2,1)S(1)}, bf16[2,8192]{1,0:T(2,128)(2,1)S(1)}, u32[]{:S(2)}, u32[]{:S(2)}) collective-permute-start(bf16[2,8192]{1,0:T(2,128)(2,1)S(1)} %get-tuple-element.41), channel_id=1, source_target_pairs={{0,96},{32,64},{64,32},{96,0},{128,224},{160,192},{192,160},{224,1... | collective-permute-start | bytes 98312 | tf_op jit(solution)/shard_map/ppermute | solution.py:273
  112.8 6.2 %collective-permute-start.30 = (bf16[2,8192]{1,0:T(2,128)(2,1)S(1)}, bf16[2,8192]{1,0:T(2,128)(2,1)S(1)}, u32[]{:S(2)}, u32[]{:S(2)}) collective-permute-start(bf16[2,8192]{1,0:T(2,128)(2,1)S(1)} %get-tuple-element.42), channel_id=1, source_target_pairs={{0,128},{32,160},{64,192},{96,224},{128,0},{160,32},{192,64},{224,... | collective-permute-start | bytes 98312 | tf_op jit(solution)/shard_map/ppermute | solution.py:273
  112.8 6.2 %collective-permute-start.31 = (bf16[2,8192]{1,0:T(2,128)(2,1)S(1)}, bf16[2,8192]{1,0:T(2,128)(2,1)S(1)}, u32[]{:S(2)}, u32[]{:S(2)}) collective-permute-start(bf16[2,8192]{1,0:T(2,128)(2,1)S(1)} %get-tuple-element.43), channel_id=1, source_target_pairs={{0,160},{32,128},{64,224},{96,192},{128,32},{160,0},{192,96},{224,... | collective-permute-start | bytes 98312 | tf_op jit(solution)/shard_map/ppermute | solution.py:273
  116.1 4.0 %collective-permute-start.32 = (bf16[2,8192]{1,0:T(2,128)(2,1)S(1)}, bf16[2,8192]{1,0:T(2,128)(2,1)S(1)}, u32[]{:S(2)}, u32[]{:S(2)}) collective-permute-start(bf16[2,8192]{1,0:T(2,128)(2,1)S(1)} %get-tuple-element.44), channel_id=1, source_target_pairs={{0,192},{32,224},{64,128},{96,160},{128,64},{160,96},{192,0},{224,... | collective-permute-start | bytes 98312 | tf_op jit(solution)/shard_map/ppermute | solution.py:273
  116.1 5.0 %collective-permute-start.33 = (bf16[2,8192]{1,0:T(2,128)(2,1)S(1)}, bf16[2,8192]{1,0:T(2,128)(2,1)S(1)}, u32[]{:S(2)}, u32[]{:S(2)}) collective-permute-start(bf16[2,8192]{1,0:T(2,128)(2,1)S(1)} %get-tuple-element.45), channel_id=1, source_target_pairs={{0,224},{32,192},{64,160},{96,128},{128,96},{160,64},{192,32},{224... | collective-permute-start | bytes 98312 | tf_op jit(solution)/shard_map/ppermute | solution.py:273

commit v2 on v1

v2 whole, which is shorter than its diff:
```python
import functools

import jax
import jax.numpy as jnp
from jax import lax
from jax.experimental import pallas as pl
from jax.experimental.pallas import tpu as pltpu
from jax.sharding import PartitionSpec as P

VOLUME = 0.03125
FIELD = (0.17101, 0.46985, -0.86603)
ROOT = (3.0 * VOLUME) ** 0.5

TILE = 256
VECS = 16
GROUP = 8
MIB = 1 << 20
WIDE = 8
TALL = 4
F32 = jnp.float32
BF16 = jnp.bfloat16

SMEM = pl.BlockSpec(memory_space=pltpu.SMEM)
VMEM = pl.BlockSpec(memory_space=pltpu.VMEM)
ANY = pl.BlockSpec(memory_space=pl.ANY)


def split3(x):
    high = x.astype(BF16).astype(F32)
    rest = x - high
    middle = rest.astype(BF16).astype(F32)
    return high, middle, rest - middle


def near_kernel(counts, pairs, stations, cells, out, station_rows, cell_rows):
    def station_chunk(i, carry):
        at = pl.ds(pl.multiple_of(i * 2048, 2048), 2048)
        x, y, z = (stations[d : d + 1, at] for d in range(3))
        station_rows[0:1, at] = x
        station_rows[1:2, at] = y
        station_rows[2:3, at] = z
        station_rows[3:4, at] = x * x + y * y + z * z
        station_rows[4:5, at] = ROOT * (FIELD[0] * x + FIELD[1] * y + FIELD[2] * z)
        station_rows[5:6, at] = jnp.ones_like(x)
        station_rows[6:8, at] = jnp.zeros((2, 2048), F32)
        return carry

    lax.fori_loop(0, stations.shape[1] // 2048, station_chunk, 0)

    def cell_chunk(i, carry):
        at = pl.ds(pl.multiple_of(i * TILE, TILE), TILE)
        x, y, z = (cells[d : d + 1, at] for d in range(3))
        zero = jnp.zeros_like(x)
        one = jnp.ones_like(x)
        square = x * x + y * y + z * z
        along = -ROOT * (FIELD[0] * x + FIELD[1] * y + FIELD[2] * z)
        lines = lax.broadcasted_iota(jnp.int32, (8, TILE), 0)

        def stack(values):
            total = jnp.zeros((8, TILE), F32)
            for line, value in values:
                total = jnp.where(lines == line, value, total)
            return total

        wide = stack(((0, -2.0 * x), (1, -2.0 * y), (2, -2.0 * z), (3, one), (5, square)))
        flat = stack(((4, one), (5, along)))
        for position, block in enumerate((wide, flat)):
            h, m, l = split3(block)
            turned = jnp.concatenate((h, h, h, m, m, l), axis=0).T
            cell_rows[i, position * TILE : (position + 1) * TILE, :] = turned.astype(BF16)
        return carry

    lax.fori_loop(0, cells.shape[1] // TILE, cell_chunk, 0)

    def step_blocks(step, carry):
        for j in range(GROUP):
            row = pairs[0, step * GROUP + j]
            column = pairs[1, step * GROUP + j]
            at = pl.ds(pl.multiple_of(row * TILE, TILE), TILE)
            h, m, l = split3(station_rows[:, at])
            right = jnp.concatenate((h, m, l, h, m, h), axis=0).astype(BF16)
            both = jnp.dot(cell_rows[column], right, preferred_element_type=F32)
            distance, along = both[:TILE], both[TILE:]
            inverse = lax.rsqrt(distance)
            square = inverse * inverse
            out[step * GROUP + j] = ((along * along * square - VOLUME) * (square * inverse)).astype(BF16)
        return carry

    lax.fori_loop(0, near_groups(counts), step_blocks, 0)


def block_mask():
    lines = lax.broadcasted_iota(jnp.int32, (GROUP * VECS, TILE), 0) // VECS
    lanes = lax.broadcasted_iota(jnp.int32, (GROUP * VECS, TILE), 1) // (TILE // GROUP)
    return lines == lanes


def near_groups(counts):
    return counts[0, lax.axis_index("cel")] // GROUP


def contract(a, b, dim):
    return lax.dot_general(a, b, (((1,), (dim,)), ((), ())), preferred_element_type=F32)


def lanes_of(column):
    return pl.ds(pl.multiple_of(column * TILE, TILE), TILE)


def place(cel, row):
    share = (row >> 2) ^ cel
    return (share & (WIDE - 1)) * TALL + (share >> 3), lanes_of(row & 3)


def forward_kernel(counts, near, mid, *refs):
    parts = refs[:4]
    u_ref, v_ref, blocks = refs[4:7]
    outs = refs[7:15]
    stacked, vectors, total = refs[15:]
    cel = lax.axis_index("cel")
    for k in range(4):
        stacked[4 * k : 4 * k + 4, :] = parts[k][...].astype(F32)
    vectors[...] = stacked[...].astype(BF16)
    total[...] = jnp.zeros_like(total)
    mask = block_mask()

    def mid_step(i, carry):
        sums = []
        for q in range(4):
            g = i * 4 + q
            source = jnp.concatenate(
                [vectors[:, lanes_of(mid[1, g * GROUP + j])] for j in range(GROUP)], axis=0
            )
            reduced = contract(source, v_ref[g], 1)
            reduced = jnp.where(mask, reduced, 0.0).astype(BF16)
            sums.append(contract(reduced, u_ref[g], 0))
        for q in range(4):
            for j in range(GROUP):
                slot, lanes = place(cel, mid[0, (i * 4 + q) * GROUP + j])
                total[slot, :, lanes] += sums[q][j * VECS : (j + 1) * VECS]
        return carry

    lax.fori_loop(0, u_ref.shape[0] // 4, mid_step, 0)

    def near_step(g, carry):
        sums = [
            contract(vectors[:, lanes_of(near[1, g * GROUP + j])], blocks[g * GROUP + j], 0)
            for j in range(GROUP)
        ]
        for j in range(GROUP):
            slot, lanes = place(cel, near[0, g * GROUP + j])
            total[slot, :, lanes] += sums[j]
        return carry

    lax.fori_loop(0, near_groups(counts), near_step, 0)
    for i in range(WIDE):
        outs[i][...] = total[TALL * i : TALL * (i + 1)].astype(outs[i].dtype)


def share_sum_kernel(own, *refs):
    parts, outs = refs[: WIDE - 1], refs[WIDE - 1 :]
    for k in range(TALL):
        total = own[k]
        for part in parts:
            total = total + part[k].astype(F32)
        outs[k][...] = total.astype(outs[k].dtype)


def weigh_kernel(own, *refs):
    parts = refs[: TALL - 1]
    weights, predicted, weighted = refs[TALL - 1 :]
    sta, cel = lax.axis_index("sta"), lax.axis_index("cel")
    total = own[...]
    for part in parts:
        total = total + part[...].astype(F32)
    share = weights[pl.ds(pl.multiple_of(cel * 8, 8), 8), :]
    for r in range(8):
        at = slice(r * 128, (r + 1) * 128)
        weighted[:, at] = (total[:, at] * share[r : r + 1, :]).astype(BF16)
    for place_of in range(8):

        @pl.when(sta == place_of)
        def _():
            for k in range(8):
                line = 2 * (k ^ place_of)
                predicted[line : line + 2, :] = total[2 * k : 2 * k + 2]


def join_kernel(*refs):
    for k in range(TALL):
        refs[TALL][k] = refs[k][...]


def adjoint_kernel(counts, near, mid, *refs):
    pieces = refs[:WIDE]
    u_ref, v_ref, blocks, kept, swapped, data, total = refs[WIDE:]
    cel = lax.axis_index("cel")
    for i in range(WIDE):
        data[TALL * i : TALL * (i + 1)] = pieces[i][...]
    total[...] = jnp.zeros_like(total)
    mask = block_mask()

    def station_tile(row):
        slot, lanes = place(cel, row)
        return data[slot, :, lanes]

    def mid_step(i, carry):
        sums = []
        for q in range(4):
            g = i * 4 + q
            source = jnp.concatenate(
                [station_tile(mid[0, g * GROUP + j]) for j in range(GROUP)], axis=0
            )
            pulled = contract(source, u_ref[g], 1)
            pulled = jnp.where(mask, pulled, 0.0).astype(BF16)
            sums.append(contract(pulled, v_ref[g], 0))
        for q in range(4):
            for j in range(GROUP):
                lanes = lanes_of(mid[1, (i * 4 + q) * GROUP + j])
                total[:, lanes] += sums[q][j * VECS : (j + 1) * VECS]
        return carry

    lax.fori_loop(0, u_ref.shape[0] // 4, mid_step, 0)

    def near_step(g, carry):
        sums = [
            contract(station_tile(near[0, g * GROUP + j]), blocks[g * GROUP + j], 1)
            for j in range(GROUP)
        ]
        for j in range(GROUP):
            total[:, lanes_of(near[1, g * GROUP + j])] += sums[j]
        return carry

    lax.fori_loop(0, near_groups(counts), near_step, 0)
    for t in range(4):
        kept[2 * t : 2 * t + 2, :] = total[4 * t : 4 * t + 2, :]
    swapped[...] = jnp.concatenate(
        [total[4 * t + 2 : 4 * t + 4, :] for t in range(4)], axis=0
    ).astype(BF16)


def chip_sum_kernel(kept, swapped, *outs):
    total = kept[...] + swapped[...].astype(F32)
    for t in range(4):
        outs[t][...] = total[2 * t : 2 * t + 2].astype(outs[t].dtype)


def params(mib):
    return pltpu.CompilerParams(vmem_limit_bytes=mib * MIB)


def body(
    model_vectors, station_xyz, cell_xyz, weights, near_pairs, near_count, mid_pairs, mid_u, mid_v
):
    slots = near_pairs.shape[2]
    near = near_pairs[0, 0].T
    mid = mid_pairs[0, 0].T
    u_factor = mid_u.reshape(-1, TILE, TILE)
    v_factor = mid_v.reshape(-1, TILE, TILE)

    def over_sta(x, k):
        return lax.ppermute(x, "sta", [(i, i ^ k) for i in range(8)])

    def over_cel(x, k):
        return lax.ppermute(x, "cel", [(i, i ^ k) for i in range(32)])

    chip_vectors = jnp.concatenate((model_vectors, over_sta(model_vectors, 1)), axis=0)
    vector_parts = [chip_vectors] + [over_sta(chip_vectors, 2 * k) for k in range(1, 4)]

    blocks = pl.pallas_call(
        near_kernel,
        in_specs=[SMEM] * 2 + [VMEM] * 2,
        out_specs=VMEM,
        out_shape=jax.ShapeDtypeStruct((slots, TILE, TILE), BF16),
        scratch_shapes=[
            pltpu.VMEM((8, station_xyz.shape[1]), F32),
            pltpu.VMEM((cell_xyz.shape[1] // TILE, 2 * TILE, 48), BF16),
        ],
        compiler_params=params(24),
        cost_estimate=pl.CostEstimate(
            flops=slots * 2 * 512 * 48 * 256, bytes_accessed=10 * MIB, transcendentals=slots * 65536
        ),
        name="near_blocks",
    )(near_count, near, station_xyz, cell_xyz)

    wide = jax.ShapeDtypeStruct((TALL, VECS, 1024), BF16)
    shares = pl.pallas_call(
        forward_kernel,
        in_specs=[SMEM] * 3 + [VMEM] * 7,
        out_specs=[VMEM] * WIDE,
        out_shape=[jax.ShapeDtypeStruct(wide.shape, F32)] + [wide] * (WIDE - 1),
        scratch_shapes=[
            pltpu.VMEM((VECS, 8192), F32),
            pltpu.VMEM((VECS, 8192), BF16),
            pltpu.VMEM((32, VECS, 1024), F32),
        ],
        compiler_params=params(24),
        name="forward",
    )(near_count, near, mid, *vector_parts, u_factor, v_factor, blocks)

    from_wide = [over_cel(shares[i], i) for i in range(1, WIDE)]
    narrow = jax.ShapeDtypeStruct((VECS, 1024), BF16)
    sums = pl.pallas_call(
        share_sum_kernel,
        in_specs=[VMEM] * WIDE,
        out_specs=[VMEM] * TALL,
        out_shape=[jax.ShapeDtypeStruct(narrow.shape, F32)] + [narrow] * (TALL - 1),
        compiler_params=params(8),
        name="share_sum",
    )(shares[0], *from_wide)
    from_tall = [over_cel(sums[k], WIDE * k) for k in range(1, TALL)]
    predicted, weighted = pl.pallas_call(
        weigh_kernel,
        in_specs=[VMEM] * (TALL + 1),
        out_specs=[VMEM] * 2,
        out_shape=[jax.ShapeDtypeStruct(narrow.shape, F32), narrow],
        compiler_params=params(4),
        name="weigh",
    )(sums[0], *from_tall, weights.reshape(-1, 128))

    gathered = [weighted] + [over_cel(weighted, WIDE * k) for k in range(1, TALL)]
    column = pl.pallas_call(
        join_kernel,
        in_specs=[VMEM] * TALL,
        out_specs=VMEM,
        out_shape=wide,
        compiler_params=params(4),
        name="join",
    )(*gathered)
    columns = [column] + [over_cel(column, i) for i in range(1, WIDE)]

    lines = jax.ShapeDtypeStruct((8, 8192), BF16)
    kept, swapped = pl.pallas_call(
        adjoint_kernel,
        in_specs=[SMEM] * 3 + [VMEM] * (WIDE + 3),
        out_specs=[VMEM] * 2,
        out_shape=[jax.ShapeDtypeStruct(lines.shape, F32), lines],
        scratch_shapes=[
            pltpu.VMEM((32, VECS, 1024), BF16),
            pltpu.VMEM((VECS, 8192), F32),
        ],
        compiler_params=params(24),
        name="adjoint",
    )(near_count, near, mid, *columns, u_factor, v_factor, blocks)
    pair = jax.ShapeDtypeStruct((2, 8192), BF16)
    terms = pl.pallas_call(
        chip_sum_kernel,
        in_specs=[VMEM] * 2,
        out_specs=[VMEM] * 4,
        out_shape=[jax.ShapeDtypeStruct(pair.shape, F32)] + [pair] * 3,
        compiler_params=params(4),
        name="chip_sum",
    )(kept, over_sta(swapped, 1))
    gradient = terms[0]
    for t in range(1, 4):
        gradient = gradient + over_sta(terms[t], 2 * t).astype(F32)
    return (predicted, gradient)


def solution(mesh):
    return jax.shard_map(
        body,
        mesh=mesh,
        in_specs=(
            P("sta", "cel"),
            P(None, "sta"),
            P(None, "cel"),
            P("sta"),
            P("sta", "cel", None, None),
            P("sta", None),
            P("sta", "cel", None, None),
            P("sta", "cel", None, None, None),
            P("sta", "cel", None, None, None),
        ),
        out_specs=(P(None, ("sta", "cel")), P("sta", "cel")),
        check_vma=False,
    )
```

time: 122 us -> 106 us (0.87)
  starting transfers between devices: 72.4 us -> 54 us
  waiting for transfers between devices: 25.4 us -> 30.7 us
  Pallas kernels: 18.4 us -> 15.8 us
    ppermute x14 -> x8, starting transfers between devices: 30.8 us -> 16.1 us  [over_sta(): return lax.ppermute(x, 'sta', [(i, i ^ k) for i in range(8)])]
    ppermute x14 -> x8, waiting for transfers between devices: 2.14 us -> 6.04 us  [over_sta(): return lax.ppermute(x, 'sta', [(i, i ^ k) for i in range(8)])]
    ppermute x20, starting transfers between devices: 41.6 us -> 37.8 us  [over_cel(): return lax.ppermute(x, 'cel', [(i, i ^ k) for i in range(32)])]
    pallas_call x6 -> x7, Pallas kernels: 18.4 us -> 15.8 us  [the longest x1 5.21 us: body(): pl.pallas_call(near_kernel, in_specs=[SMEM] * 2 + [VMEM] * 2, out_specs=V...]
    ppermute x20, waiting for transfers between devices: 23.3 us -> 24.7 us  [over_cel(): return lax.ppermute(x, 'cel', [(i, i ^ k) for i in range(32)])]
    unnamed x20 -> x16, local copies, waits for them, and re-layouts: 2.66 us -> 3.3 us
  transfers between devices with their start and end apart: 34 -> 28, of which waited for: 11 -> 16; matrix products, arithmetic and copies ran while one was open for 1% -> 0% of each run, Pallas kernels for 5% -> 5%
where the time goes in v2:
time: 106 us
  starting transfers between devices  54 us (51%)
  waiting for transfers between devices  30.7 us (29%)
  Pallas kernels  15.8 us (15%)
  local copies, waits for them, and re-layouts  3.3 us (3%)
  other arithmetic  1.52 us (1%)
    ppermute x20, starting transfers between devices, over_cel(): return lax.ppermute(x, 'cel', [(i, i ^ k) for i in range(32)])  37.8 us
    ppermute x20, waiting for transfers between devices, over_cel(): return lax.ppermute(x, 'cel', [(i, i ^ k) for i in range(32)])  24.7 us
    ppermute x8, starting transfers between devices, over_sta(): return lax.ppermute(x, 'sta', [(i, i ^ k) for i in range(8)])  16.1 us
    ppermute x8, waiting for transfers between devices, over_sta(): return lax.ppermute(x, 'sta', [(i, i ^ k) for i in range(8)])  6.04 us
    pallas_call x1, Pallas kernels, body(): pl.pallas_call(near_kernel, in_specs=[SMEM] * 2 + [VMEM] * 2, out_specs=V...  5.21 us
    pallas_call x1, Pallas kernels, body(): pl.pallas_call(adjoint_kernel, in_specs=[SMEM] * 3 + [VMEM] * (WIDE + 3),...  4.87 us
    pallas_call x1, Pallas kernels, body(): pl.pallas_call(forward_kernel, in_specs=[SMEM] * 3 + [VMEM] * 7, out_spec...  4.8 us
    unnamed x16, local copies, waits for them, and re-layouts  3.3 us
  transfers between devices with their start and end apart: 28, of which 16 were waited for; matrix products, arithmetic and copies ran while one was open for 0% of the time, Pallas kernels for 5%

profile of v2, /device:TPU:1, one launch (start us, length us, event | category | flops | bytes accessed | tf_op | source)
XLA Modules:
  0.0 106.0 jit_solution(4366939097465091099)
XLA Ops:
  0.6 3.3 %collective-permute-start = (bf16[2,8192]{1,0:T(2,128)(2,1)}, bf16[2,8192]{1,0:T(2,128)(2,1)S(1)}, u32[]{:S(2)}, u32[]{:S(2)}) collective-permute-start(bf16[2,8192]{1,0:T(2,128)(2,1)} %param.9), channel_id=1, source_target_pairs={{0,32},{32,0},{64,96},{96,64},{128,160},{160,128},{192,224},{224,1... | collective-permute-start | bytes 98312 | tf_op jit(solution)/shard_map/ppermute | solution.py:262
  4.0 1.1 %collective-permute-done = bf16[2,8192]{1,0:T(2,128)(2,1)S(1)} collective-permute-done((bf16[2,8192]{1,0:T(2,128)(2,1)}, bf16[2,8192]{1,0:T(2,128)(2,1)S(1)}, u32[]{:S(2)}, u32[]{:S(2)}) %collective-permute-start) | collective-permute-done | bytes 32800 | tf_op jit(solution)/shard_map/ppermute | solution.py:262
  5.0 0.8 pad_maximum_fusion.refs_0_
  5.9 0.8 collective-permute-start.3
  6.7 0.5 collective-permute-start.2
  7.2 2.0 %collective-permute-start.1 = (bf16[4,8192]{1,0:T(4,128)(2,1)S(1)}, bf16[4,8192]{1,0:T(4,128)(2,1)S(1)}, u32[]{:S(2)}, u32[]{:S(2)}) collective-permute-start(bf16[4,8192]{1,0:T(4,128)(2,1)S(1)} %pad_maximum_fusion.refs_0_), channel_id=1, source_target_pairs={{0,64},{32,96},{64,0},{96,32},{128,192},{160,224},{192,128},{224,1... | collective-permute-start | bytes 196616 | tf_op jit(solution)/shard_map/ppermute | solution.py:262
  9.2 1.0 copy-done.2
  10.2 0.9 copy-done.3
  11.2 0.7 copy-done.5
  11.8 0.7 copy-done.6
  12.5 5.2 %near_blocks.1.refs_6_.refs_10_ = bf16[64,256,256]{2,1,0:T(8,128)(2,1)S(1)} custom-call(s32[1,32]{1,0:T(1,128)S(1)} %copy-done.6, s32[2,64]{1,0:T(2,128)S(1)} %bitcast.14, f32[3,32768]{1,0:T(4,128)S(1)} %copy-done.2, f32[3,8192]{1,0:T(4,128)S(1)} %copy-done.3), custom_call_target="tpu_custom_call" | custom-call | flops 805306368 | bytes 10485760 | tf_op jit(solution)/shard_map/near_blocks/pallas_call | solution.py:270
  17.8 4.8 %forward.1 = (f32[4,16,1024]{2,1,0:T(8,128)S(1)}, bf16[4,16,1024]{2,1,0:T(8,128)(2,1)S(1)}, bf16[4,16,1024]{2,1,0:T(8,128)(2,1)S(1)}, bf16[4,16,1024]{2,1,0:T(8,...) custom-call(s32[1,32]{1,0:T(1,128)S(1)} %copy-done.6, ...), custom_call_target="tpu_custom_call" | custom-call | tf_op jit(solution)/shard_map/forward/pallas_call | solution.py:287
  22.6 2.7 %collective-permute-start.4 = (bf16[4,16,1024]{2,1,0:T(8,128)(2,1)S(1)}, bf16[4,16,1024]{2,1,0:T(8,128)(2,1)S(1)}, u32[]{:S(2)}, u32[]{:S(2)}) collective-permute-start(bf16[4,16,1024]{2,1,0:T(8,128)(2,1)S(1)} %get-tuple-element.23), channel_id=1, source_target_pairs={{0,1},{1,0},{2,3},{3,2},{4,5},{5,4},{6,7},{7,6},{8,9},{9,8},{10,11... | collective-permute-start | bytes 393224 | tf_op jit(solution)/shard_map/ppermute | solution.py:265
  25.3 5.8 %collective-permute-start.5 = (bf16[4,16,1024]{2,1,0:T(8,128)(2,1)S(1)}, bf16[4,16,1024]{2,1,0:T(8,128)(2,1)S(1)}, u32[]{:S(2)}, u32[]{:S(2)}) collective-permute-start(bf16[4,16,1024]{2,1,0:T(8,128)(2,1)S(1)} %get-tuple-element.24), channel_id=1, source_target_pairs={{0,2},{1,3},{2,0},{3,1},{4,6},{5,7},{6,4},{7,5},{8,10},{9,11},{10,... | collective-permute-start | bytes 393224 | tf_op jit(solution)/shard_map/ppermute | solution.py:265
  31.1 0.2 collective-permute-start.6
  31.3 2.3 %collective-permute-start.7 = (bf16[4,16,1024]{2,1,0:T(8,128)(2,1)S(1)}, bf16[4,16,1024]{2,1,0:T(8,128)(2,1)S(1)}, u32[]{:S(2)}, u32[]{:S(2)}) collective-permute-start(bf16[4,16,1024]{2,1,0:T(8,128)(2,1)S(1)} %get-tuple-element.26), channel_id=1, source_target_pairs={{0,4},{1,5},{2,6},{3,7},{4,0},{5,1},{6,2},{7,3},{8,12},{9,13},{10,... | collective-permute-start | bytes 393224 | tf_op jit(solution)/shard_map/ppermute | solution.py:265
  33.6 3.9 %collective-permute-start.9 = (bf16[4,16,1024]{2,1,0:T(8,128)(2,1)S(1)}, bf16[4,16,1024]{2,1,0:T(8,128)(2,1)S(1)}, u32[]{:S(2)}, u32[]{:S(2)}) collective-permute-start(bf16[4,16,1024]{2,1,0:T(8,128)(2,1)S(1)} %get-tuple-element.28), channel_id=1, source_target_pairs={{0,6},{1,7},{2,4},{3,5},{4,2},{5,3},{6,0},{7,1},{8,14},{9,15},{10,... | collective-permute-start | bytes 393224 | tf_op jit(solution)/shard_map/ppermute | solution.py:265
  37.5 1.0 collective-permute-start.10
  38.5 0.8 collective-permute-done.8.refs_4_
  39.3 4.4 %collective-permute-done.9.refs_5_ = bf16[4,16,1024]{2,1,0:T(8,128)(2,1)S(1)} collective-permute-done((bf16[4,16,1024]{2,1,0:T(8,128)(2,1)S(1)}, bf16[4,16,1024]{2,1,0:T(8,128)(2,1)S(1)}, u32[]{:S(2)}, u32[]{:S(2)}) %collective-permute-start.9) | collective-permute-done | bytes 131104 | tf_op jit(solution)/shard_map/ppermute | solution.py:265
  43.7 1.9 %collective-permute-done.10.refs_6_ = bf16[4,16,1024]{2,1,0:T(8,128)(2,1)S(1)} collective-permute-done((bf16[4,16,1024]{2,1,0:T(8,128)(2,1)S(1)}, bf16[4,16,1024]{2,1,0:T(8,128)(2,1)S(1)}, u32[]{:S(2)}, u32[]{:S(2)}) %collective-permute-start.10) | collective-permute-done | bytes 131104 | tf_op jit(solution)/shard_map/ppermute | solution.py:265
  45.8 9.1 %collective-permute-start.12 = (bf16[16,1024]{1,0:T(8,128)(2,1)S(1)}, bf16[16,1024]{1,0:T(8,128)(2,1)S(1)}, u32[]{:S(2)}, u32[]{:S(2)}) collective-permute-start(bf16[16,1024]{1,0:T(8,128)(2,1)S(1)} %get-tuple-element.32), channel_id=1, source_target_pairs={{0,16},{1,17},{2,18},{3,19},{4,20},{5,21},{6,22},{7,23},{8,24},{9,... | collective-permute-start | bytes 98312 | tf_op jit(solution)/shard_map/ppermute | solution.py:265
  54.9 0.2 collective-permute-start.13
  55.1 1.5 %collective-permute-done.12.refs_1_ = bf16[16,1024]{1,0:T(8,128)(2,1)S(1)} collective-permute-done((bf16[16,1024]{1,0:T(8,128)(2,1)S(1)}, bf16[16,1024]{1,0:T(8,128)(2,1)S(1)}, u32[]{:S(2)}, u32[]{:S(2)}) %collective-permute-start.12) | collective-permute-done | bytes 32800 | tf_op jit(solution)/shard_map/ppermute | solution.py:265
  56.6 3.2 %collective-permute-done.13.refs_2_ = bf16[16,1024]{1,0:T(8,128)(2,1)S(1)} collective-permute-done((bf16[16,1024]{1,0:T(8,128)(2,1)S(1)}, bf16[16,1024]{1,0:T(8,128)(2,1)S(1)}, u32[]{:S(2)}, u32[]{:S(2)}) %collective-permute-start.13) | collective-permute-done | bytes 32800 | tf_op jit(solution)/shard_map/ppermute | solution.py:265
  59.8 0.7 weigh.1
  60.5 2.2 %collective-permute-start.16 = (bf16[16,1024]{1,0:T(8,128)(2,1)S(1)}, bf16[16,1024]{1,0:T(8,128)(2,1)S(1)}, u32[]{:S(2)}, u32[]{:S(2)}) collective-permute-start(bf16[16,1024]{1,0:T(8,128)(2,1)S(1)} %get-tuple-element.35.refs_0_), channel_id=1, source_target_pairs={{0,24},{1,25},{2,26},{3,27},{4,28},{5,29},{6,30},{7,31},{8,16},{9,... | collective-permute-start | bytes 98312 | tf_op jit(solution)/shard_map/ppermute | solution.py:265
  62.7 3.3 %collective-permute-start.15 = (bf16[16,1024]{1,0:T(8,128)(2,1)S(1)}, bf16[16,1024]{1,0:T(8,128)(2,1)S(1)}, u32[]{:S(2)}, u32[]{:S(2)}) collective-permute-start(bf16[16,1024]{1,0:T(8,128)(2,1)S(1)} %get-tuple-element.35.refs_0_), channel_id=1, source_target_pairs={{0,16},{1,17},{2,18},{3,19},{4,20},{5,21},{6,22},{7,23},{8,24},{9,... | collective-permute-start | bytes 98312 | tf_op jit(solution)/shard_map/ppermute | solution.py:265
  66.2 3.3 %collective-permute-done.15.refs_2_ = bf16[16,1024]{1,0:T(8,128)(2,1)S(1)} collective-permute-done((bf16[16,1024]{1,0:T(8,128)(2,1)S(1)}, bf16[16,1024]{1,0:T(8,128)(2,1)S(1)}, u32[]{:S(2)}, u32[]{:S(2)}) %collective-permute-start.15) | collective-permute-done | bytes 32800 | tf_op jit(solution)/shard_map/ppermute | solution.py:265
  69.4 0.6 collective-permute-done.14.refs_1_
  70.0 0.3 collective-permute-start.23
  70.3 0.3 collective-permute-start.22
  70.6 2.2 %collective-permute-start.21 = (bf16[4,16,1024]{2,1,0:T(8,128)(2,1)S(1)}, bf16[4,16,1024]{2,1,0:T(8,128)(2,1)S(1)}, u32[]{:S(2)}, u32[]{:S(2)}) collective-permute-start(bf16[4,16,1024]{2,1,0:T(8,128)(2,1)S(1)} %join.1.refs_0_), channel_id=1, source_target_pairs={{0,5},{1,4},{2,7},{3,6},{4,1},{5,0},{6,3},{7,2},{8,13},{9,12},{10,... | collective-permute-start | bytes 393224 | tf_op jit(solution)/shard_map/ppermute | solution.py:265
  72.8 2.9 %collective-permute-start.20 = (bf16[4,16,1024]{2,1,0:T(8,128)(2,1)S(1)}, bf16[4,16,1024]{2,1,0:T(8,128)(2,1)S(1)}, u32[]{:S(2)}, u32[]{:S(2)}) collective-permute-start(bf16[4,16,1024]{2,1,0:T(8,128)(2,1)S(1)} %join.1.refs_0_), channel_id=1, source_target_pairs={{0,4},{1,5},{2,6},{3,7},{4,0},{5,1},{6,2},{7,3},{8,12},{9,13},{10,... | collective-permute-start | bytes 393224 | tf_op jit(solution)/shard_map/ppermute | solution.py:265
  75.6 1.6 %collective-permute-done.23.refs_7_ = bf16[4,16,1024]{2,1,0:T(8,128)(2,1)S(1)} collective-permute-done((bf16[4,16,1024]{2,1,0:T(8,128)(2,1)S(1)}, bf16[4,16,1024]{2,1,0:T(8,128)(2,1)S(1)}, u32[]{:S(2)}, u32[]{:S(2)}) %collective-permute-start.23) | collective-permute-done | bytes 131104 | tf_op jit(solution)/shard_map/ppermute | solution.py:265
  77.2 0.4 collective-permute-done.22.refs_6_
  77.6 1.3 %collective-permute-start.17 = (bf16[4,16,1024]{2,1,0:T(8,128)(2,1)S(1)}, bf16[4,16,1024]{2,1,0:T(8,128)(2,1)S(1)}, u32[]{:S(2)}, u32[]{:S(2)}) collective-permute-start(bf16[4,16,1024]{2,1,0:T(8,128)(2,1)S(1)} %join.1.refs_0_), channel_id=1, source_target_pairs={{0,1},{1,0},{2,3},{3,2},{4,5},{5,4},{6,7},{7,6},{8,9},{9,8},{10,11... | collective-permute-start | bytes 393224 | tf_op jit(solution)/shard_map/ppermute | solution.py:265
  78.9 3.2 %collective-permute-done.20.refs_4_ = bf16[4,16,1024]{2,1,0:T(8,128)(2,1)S(1)} collective-permute-done((bf16[4,16,1024]{2,1,0:T(8,128)(2,1)S(1)}, bf16[4,16,1024]{2,1,0:T(8,128)(2,1)S(1)}, u32[]{:S(2)}, u32[]{:S(2)}) %collective-permute-start.20) | collective-permute-done | bytes 131104 | tf_op jit(solution)/shard_map/ppermute | solution.py:265
  82.1 1.5 %collective-permute-done.19.refs_3_ = bf16[4,16,1024]{2,1,0:T(8,128)(2,1)S(1)} collective-permute-done((bf16[4,16,1024]{2,1,0:T(8,128)(2,1)S(1)}, bf16[4,16,1024]{2,1,0:T(8,128)(2,1)S(1)}, u32[]{:S(2)}, u32[]{:S(2)}) %collective-permute-start.19) | collective-permute-done | bytes 131104 | tf_op jit(solution)/shard_map/ppermute | solution.py:265
  83.6 2.4 %collective-permute-done.18.refs_2_ = bf16[4,16,1024]{2,1,0:T(8,128)(2,1)S(1)} collective-permute-done((bf16[4,16,1024]{2,1,0:T(8,128)(2,1)S(1)}, bf16[4,16,1024]{2,1,0:T(8,128)(2,1)S(1)}, u32[]{:S(2)}, u32[]{:S(2)}) %collective-permute-start.18) | collective-permute-done | bytes 131104 | tf_op jit(solution)/shard_map/ppermute | solution.py:265
  86.0 4.9 %adjoint.1 = (f32[8,8192]{1,0:T(8,128)S(1)}, bf16[8,8192]{1,0:T(8,128)(2,1)S(1)}) custom-call(s32[1,32]{1,0:T(1,128)S(1)} %copy-done.6, s32[2,64]{1,0:T(2,128)S(1)} %bitcast.16, s32[2,128]{1,0:T(2,128)S(1)} %bitcast.18, bf16[4,16,1024]{2,1,0:T(8,128)(2,1)S(1)} %join.1.refs_0_, bf16[4,16,1024]{2,1,0:T(8,128)(2,1)S(1)} %collective-permute-done.17.refs_1_, ...), custom_call_target="tpu_custom_call" | custom-call | tf_op jit(solution)/shard_map/adjoint/pallas_call | solution.py:333
  90.9 5.1 %collective-permute-start.24 = (bf16[8,8192]{1,0:T(8,128)(2,1)S(1)}, bf16[8,8192]{1,0:T(8,128)(2,1)S(1)}, u32[]{:S(2)}, u32[]{:S(2)}) collective-permute-start(bf16[8,8192]{1,0:T(8,128)(2,1)S(1)} %get-tuple-element.37), channel_id=1, source_target_pairs={{0,32},{32,0},{64,96},{96,64},{128,160},{160,128},{192,224},{224,1... | collective-permute-start | bytes 393224 | tf_op jit(solution)/shard_map/ppermute | solution.py:262
  96.0 1.0 collective-permute-done.24.swapped
  97.0 0.3 collective-permute-start.25
  97.3 4.1 %collective-permute-start.26 = (bf16[2,8192]{1,0:T(2,128)(2,1)S(1)}, bf16[2,8192]{1,0:T(2,128)(2,1)S(1)}, u32[]{:S(2)}, u32[]{:S(2)}) collective-permute-start(bf16[2,8192]{1,0:T(2,128)(2,1)S(1)} %get-tuple-element.40), channel_id=1, source_target_pairs={{0,128},{32,160},{64,192},{96,224},{128,0},{160,32},{192,64},{224,... | collective-permute-start | bytes 98312 | tf_op jit(solution)/shard_map/ppermute | solution.py:262
  101.4 1.6 %collective-permute-done.26 = bf16[2,8192]{1,0:T(2,128)(2,1)S(1)} collective-permute-done((bf16[2,8192]{1,0:T(2,128)(2,1)S(1)}, bf16[2,8192]{1,0:T(2,128)(2,1)S(1)}, u32[]{:S(2)}, u32[]{:S(2)}) %collective-permute-start.26) | collective-permute-done | bytes 32800 | tf_op jit(solution)/shard_map/ppermute | solution.py:262
  103.0 2.3 %collective-permute-done.27 = bf16[2,8192]{1,0:T(2,128)(2,1)S(1)} collective-permute-done((bf16[2,8192]{1,0:T(2,128)(2,1)S(1)}, bf16[2,8192]{1,0:T(2,128)(2,1)S(1)}, u32[]{:S(2)}, u32[]{:S(2)}) %collective-permute-start.27) | collective-permute-done | bytes 32800 | tf_op jit(solution)/shard_map/ppermute | solution.py:262
  105.4 0.7 convert_add_fusion
  (33 shorter events, 0.5 us)
Async XLA Ops:
  0.6 4.4 %collective-permute-start = (bf16[2,8192]{1,0:T(2,128)(2,1)}, bf16[2,8192]{1,0:T(2,128)(2,1)S(1)}, u32[]{:S(2)}, u32[]{:S(2)}) collective-permute-start(bf16[2,8192]{1,0:T(2,128)(2,1)} %param.9), channel_id=1, source_target_pairs={{0,32},{32,0},{64,96},{96,64},{128,160},{160,128},{192,224},{224,1... | collective-permute-start | bytes 98312 | tf_op jit(solution)/shard_map/ppermute | solution.py:262
  5.9 11.8 %collective-permute-start.3 = (bf16[4,8192]{1,0:T(4,128)(2,1)S(1)}, bf16[4,8192]{1,0:T(4,128)(2,1)S(1)}, u32[]{:S(2)}, u32[]{:S(2)}) collective-permute-start(bf16[4,8192]{1,0:T(4,128)(2,1)S(1)} %pad_maximum_fusion.refs_0_), channel_id=1, source_target_pairs={{0,192},{32,224},{64,128},{96,160},{128,64},{160,96},{192,0},{224,... | collective-permute-start | bytes 196616 | tf_op jit(solution)/shard_map/ppermute | solution.py:262
  6.7 11.0 %collective-permute-start.2 = (bf16[4,8192]{1,0:T(4,128)(2,1)S(1)}, bf16[4,8192]{1,0:T(4,128)(2,1)S(1)}, u32[]{:S(2)}, u32[]{:S(2)}) collective-permute-start(bf16[4,8192]{1,0:T(4,128)(2,1)S(1)} %pad_maximum_fusion.refs_0_), channel_id=1, source_target_pairs={{0,128},{32,160},{64,192},{96,224},{128,0},{160,32},{192,64},{224,... | collective-permute-start | bytes 196616 | tf_op jit(solution)/shard_map/ppermute | solution.py:262
  7.2 10.5 %collective-permute-start.1 = (bf16[4,8192]{1,0:T(4,128)(2,1)S(1)}, bf16[4,8192]{1,0:T(4,128)(2,1)S(1)}, u32[]{:S(2)}, u32[]{:S(2)}) collective-permute-start(bf16[4,8192]{1,0:T(4,128)(2,1)S(1)} %pad_maximum_fusion.refs_0_), channel_id=1, source_target_pairs={{0,64},{32,96},{64,0},{96,32},{128,192},{160,224},{192,128},{224,1... | collective-permute-start | bytes 196616 | tf_op jit(solution)/shard_map/ppermute | solution.py:262
  9.2 1.0 copy-start.2
  10.2 0.9 copy-start.3
  11.1 0.7 copy-start.5
  11.8 0.7 copy-start.6
  12.5 5.3 %copy-start = (bf16[1,1,128,32,256]{4,3,2,1,0:T(8,128)(2,1)S(1)}, bf16[1,1,128,32,256]{4,3,2,1,0:T(8,128)(2,1)}, u32[]{:S(2)}) copy-start(bf16[1,1,128,32,256]{4,3,2,1,0:T(8,128)(2,1)} %param.16) | copy-start | bytes 6291460
  12.5 5.3 %copy-start.1 = (bf16[1,1,128,32,256]{4,3,2,1,0:T(8,128)(2,1)S(1)}, bf16[1,1,128,32,256]{4,3,2,1,0:T(8,128)(2,1)}, u32[]{:S(2)}) copy-start(bf16[1,1,128,32,256]{4,3,2,1,0:T(8,128)(2,1)} %param.17) | copy-start | bytes 6291460
  12.5 5.3 %copy-start.7 = (s32[1,1,128,2]{2,3,1,0:T(2,128)S(1)}, s32[1,1,128,2]{2,3,1,0:T(2,128)}, u32[]{:S(2)}) copy-start(s32[1,1,128,2]{2,3,1,0:T(2,128)} %param.15) | copy-start | bytes 3076
  17.8 42.0 %copy-start.4 = (f32[32768]{0:T(1024)S(1)}, f32[32768]{0:T(1024)}, u32[]{:S(2)}) copy-start(f32[32768]{0:T(1024)} %param.12) | copy-start | bytes 393220
  22.6 11.0 %collective-permute-start.4 = (bf16[4,16,1024]{2,1,0:T(8,128)(2,1)S(1)}, bf16[4,16,1024]{2,1,0:T(8,128)(2,1)S(1)}, u32[]{:S(2)}, u32[]{:S(2)}) collective-permute-start(bf16[4,16,1024]{2,1,0:T(8,128)(2,1)S(1)} %get-tuple-element.23), channel_id=1, source_target_pairs={{0,1},{1,0},{2,3},{3,2},{4,5},{5,4},{6,7},{7,6},{8,9},{9,8},{10,11... | collective-permute-start | bytes 393224 | tf_op jit(solution)/shard_map/ppermute | solution.py:265
  25.3 12.2 %collective-permute-start.5 = (bf16[4,16,1024]{2,1,0:T(8,128)(2,1)S(1)}, bf16[4,16,1024]{2,1,0:T(8,128)(2,1)S(1)}, u32[]{:S(2)}, u32[]{:S(2)}) collective-permute-start(bf16[4,16,1024]{2,1,0:T(8,128)(2,1)S(1)} %get-tuple-element.24), channel_id=1, source_target_pairs={{0,2},{1,3},{2,0},{3,1},{4,6},{5,7},{6,4},{7,5},{8,10},{9,11},{10,... | collective-permute-start | bytes 393224 | tf_op jit(solution)/shard_map/ppermute | solution.py:265
  31.1 7.5 %collective-permute-start.6 = (bf16[4,16,1024]{2,1,0:T(8,128)(2,1)S(1)}, bf16[4,16,1024]{2,1,0:T(8,128)(2,1)S(1)}, u32[]{:S(2)}, u32[]{:S(2)}) collective-permute-start(bf16[4,16,1024]{2,1,0:T(8,128)(2,1)S(1)} %get-tuple-element.25), channel_id=1, source_target_pairs={{0,3},{1,2},{2,1},{3,0},{4,7},{5,6},{6,5},{7,4},{8,11},{9,10},{10,... | collective-permute-start | bytes 393224 | tf_op jit(solution)/shard_map/ppermute | solution.py:265
  31.3 7.3 %collective-permute-start.7 = (bf16[4,16,1024]{2,1,0:T(8,128)(2,1)S(1)}, bf16[4,16,1024]{2,1,0:T(8,128)(2,1)S(1)}, u32[]{:S(2)}, u32[]{:S(2)}) collective-permute-start(bf16[4,16,1024]{2,1,0:T(8,128)(2,1)S(1)} %get-tuple-element.26), channel_id=1, source_target_pairs={{0,4},{1,5},{2,6},{3,7},{4,0},{5,1},{6,2},{7,3},{8,12},{9,13},{10,... | collective-permute-start | bytes 393224 | tf_op jit(solution)/shard_map/ppermute | solution.py:265
  33.6 5.8 %collective-permute-start.8 = (bf16[4,16,1024]{2,1,0:T(8,128)(2,1)S(1)}, bf16[4,16,1024]{2,1,0:T(8,128)(2,1)S(1)}, u32[]{:S(2)}, u32[]{:S(2)}) collective-permute-start(bf16[4,16,1024]{2,1,0:T(8,128)(2,1)S(1)} %get-tuple-element.27), channel_id=1, source_target_pairs={{0,5},{1,4},{2,7},{3,6},{4,1},{5,0},{6,3},{7,2},{8,13},{9,12},{10,... | collective-permute-start | bytes 393224 | tf_op jit(solution)/shard_map/ppermute | solution.py:265
  33.6 10.2 %collective-permute-start.9 = (bf16[4,16,1024]{2,1,0:T(8,128)(2,1)S(1)}, bf16[4,16,1024]{2,1,0:T(8,128)(2,1)S(1)}, u32[]{:S(2)}, u32[]{:S(2)}) collective-permute-start(bf16[4,16,1024]{2,1,0:T(8,128)(2,1)S(1)} %get-tuple-element.28), channel_id=1, source_target_pairs={{0,6},{1,7},{2,4},{3,5},{4,2},{5,3},{6,0},{7,1},{8,14},{9,15},{10,... | collective-permute-start | bytes 393224 | tf_op jit(solution)/shard_map/ppermute | solution.py:265
  37.5 8.1 %collective-permute-start.10 = (bf16[4,16,1024]{2,1,0:T(8,128)(2,1)S(1)}, bf16[4,16,1024]{2,1,0:T(8,128)(2,1)S(1)}, u32[]{:S(2)}, u32[]{:S(2)}) collective-permute-start(bf16[4,16,1024]{2,1,0:T(8,128)(2,1)S(1)} %get-tuple-element.29), channel_id=1, source_target_pairs={{0,7},{1,6},{2,5},{3,4},{4,3},{5,2},{6,1},{7,0},{8,15},{9,14},{10,... | collective-permute-start | bytes 393224 | tf_op jit(solution)/shard_map/ppermute | solution.py:265
  45.7 9.4 %collective-permute-start.11 = (bf16[16,1024]{1,0:T(8,128)(2,1)S(1)}, bf16[16,1024]{1,0:T(8,128)(2,1)S(1)}, u32[]{:S(2)}, u32[]{:S(2)}) collective-permute-start(bf16[16,1024]{1,0:T(8,128)(2,1)S(1)} %get-tuple-element.31), channel_id=1, source_target_pairs={{0,8},{1,9},{2,10},{3,11},{4,12},{5,13},{6,14},{7,15},{8,0},{9,1},... | collective-permute-start | bytes 98312 | tf_op jit(solution)/shard_map/ppermute | solution.py:265
  45.8 10.8 %collective-permute-start.12 = (bf16[16,1024]{1,0:T(8,128)(2,1)S(1)}, bf16[16,1024]{1,0:T(8,128)(2,1)S(1)}, u32[]{:S(2)}, u32[]{:S(2)}) collective-permute-start(bf16[16,1024]{1,0:T(8,128)(2,1)S(1)} %get-tuple-element.32), channel_id=1, source_target_pairs={{0,16},{1,17},{2,18},{3,19},{4,20},{5,21},{6,22},{7,23},{8,24},{9,... | collective-permute-start | bytes 98312 | tf_op jit(solution)/shard_map/ppermute | solution.py:265
  54.9 4.9 %collective-permute-start.13 = (bf16[16,1024]{1,0:T(8,128)(2,1)S(1)}, bf16[16,1024]{1,0:T(8,128)(2,1)S(1)}, u32[]{:S(2)}, u32[]{:S(2)}) collective-permute-start(bf16[16,1024]{1,0:T(8,128)(2,1)S(1)} %get-tuple-element.33), channel_id=1, source_target_pairs={{0,24},{1,25},{2,26},{3,27},{4,28},{5,29},{6,30},{7,31},{8,16},{9,... | collective-permute-start | bytes 98312 | tf_op jit(solution)/shard_map/ppermute | solution.py:265
  60.5 5.7 %collective-permute-start.16 = (bf16[16,1024]{1,0:T(8,128)(2,1)S(1)}, bf16[16,1024]{1,0:T(8,128)(2,1)S(1)}, u32[]{:S(2)}, u32[]{:S(2)}) collective-permute-start(bf16[16,1024]{1,0:T(8,128)(2,1)S(1)} %get-tuple-element.35.refs_0_), channel_id=1, source_target_pairs={{0,24},{1,25},{2,26},{3,27},{4,28},{5,29},{6,30},{7,31},{8,16},{9,... | collective-permute-start | bytes 98312 | tf_op jit(solution)/shard_map/ppermute | solution.py:265
  62.7 6.7 %collective-permute-start.15 = (bf16[16,1024]{1,0:T(8,128)(2,1)S(1)}, bf16[16,1024]{1,0:T(8,128)(2,1)S(1)}, u32[]{:S(2)}, u32[]{:S(2)}) collective-permute-start(bf16[16,1024]{1,0:T(8,128)(2,1)S(1)} %get-tuple-element.35.refs_0_), channel_id=1, source_target_pairs={{0,16},{1,17},{2,18},{3,19},{4,20},{5,21},{6,22},{7,23},{8,24},{9,... | collective-permute-start | bytes 98312 | tf_op jit(solution)/shard_map/ppermute | solution.py:265
  66.1 4.0 %collective-permute-start.14 = (bf16[16,1024]{1,0:T(8,128)(2,1)S(1)}, bf16[16,1024]{1,0:T(8,128)(2,1)S(1)}, u32[]{:S(2)}, u32[]{:S(2)}) collective-permute-start(bf16[16,1024]{1,0:T(8,128)(2,1)S(1)} %get-tuple-element.35.refs_0_), channel_id=1, source_target_pairs={{0,8},{1,9},{2,10},{3,11},{4,12},{5,13},{6,14},{7,15},{8,0},{9,1},... | collective-permute-start | bytes 98312 | tf_op jit(solution)/shard_map/ppermute | solution.py:265
  70.0 7.2 %collective-permute-start.23 = (bf16[4,16,1024]{2,1,0:T(8,128)(2,1)S(1)}, bf16[4,16,1024]{2,1,0:T(8,128)(2,1)S(1)}, u32[]{:S(2)}, u32[]{:S(2)}) collective-permute-start(bf16[4,16,1024]{2,1,0:T(8,128)(2,1)S(1)} %join.1.refs_0_), channel_id=1, source_target_pairs={{0,7},{1,6},{2,5},{3,4},{4,3},{5,2},{6,1},{7,0},{8,15},{9,14},{10,... | collective-permute-start | bytes 393224 | tf_op jit(solution)/shard_map/ppermute | solution.py:265
  70.3 7.3 %collective-permute-start.22 = (bf16[4,16,1024]{2,1,0:T(8,128)(2,1)S(1)}, bf16[4,16,1024]{2,1,0:T(8,128)(2,1)S(1)}, u32[]{:S(2)}, u32[]{:S(2)}) collective-permute-start(bf16[4,16,1024]{2,1,0:T(8,128)(2,1)S(1)} %join.1.refs_0_), channel_id=1, source_target_pairs={{0,6},{1,7},{2,4},{3,5},{4,2},{5,3},{6,0},{7,1},{8,14},{9,15},{10,... | collective-permute-start | bytes 393224 | tf_op jit(solution)/shard_map/ppermute | solution.py:265
  70.6 8.3 %collective-permute-start.21 = (bf16[4,16,1024]{2,1,0:T(8,128)(2,1)S(1)}, bf16[4,16,1024]{2,1,0:T(8,128)(2,1)S(1)}, u32[]{:S(2)}, u32[]{:S(2)}) collective-permute-start(bf16[4,16,1024]{2,1,0:T(8,128)(2,1)S(1)} %join.1.refs_0_), channel_id=1, source_target_pairs={{0,5},{1,4},{2,7},{3,6},{4,1},{5,0},{6,3},{7,2},{8,13},{9,12},{10,... | collective-permute-start | bytes 393224 | tf_op jit(solution)/shard_map/ppermute | solution.py:265
  72.8 9.3 %collective-permute-start.20 = (bf16[4,16,1024]{2,1,0:T(8,128)(2,1)S(1)}, bf16[4,16,1024]{2,1,0:T(8,128)(2,1)S(1)}, u32[]{:S(2)}, u32[]{:S(2)}) collective-permute-start(bf16[4,16,1024]{2,1,0:T(8,128)(2,1)S(1)} %join.1.refs_0_), channel_id=1, source_target_pairs={{0,4},{1,5},{2,6},{3,7},{4,0},{5,1},{6,2},{7,3},{8,12},{9,13},{10,... | collective-permute-start | bytes 393224 | tf_op jit(solution)/shard_map/ppermute | solution.py:265
  75.6 8.0 %collective-permute-start.19 = (bf16[4,16,1024]{2,1,0:T(8,128)(2,1)S(1)}, bf16[4,16,1024]{2,1,0:T(8,128)(2,1)S(1)}, u32[]{:S(2)}, u32[]{:S(2)}) collective-permute-start(bf16[4,16,1024]{2,1,0:T(8,128)(2,1)S(1)} %join.1.refs_0_), channel_id=1, source_target_pairs={{0,3},{1,2},{2,1},{3,0},{4,7},{5,6},{6,5},{7,4},{8,11},{9,10},{10,... | collective-permute-start | bytes 393224 | tf_op jit(solution)/shard_map/ppermute | solution.py:265
  77.2 8.7 %collective-permute-start.18 = (bf16[4,16,1024]{2,1,0:T(8,128)(2,1)S(1)}, bf16[4,16,1024]{2,1,0:T(8,128)(2,1)S(1)}, u32[]{:S(2)}, u32[]{:S(2)}) collective-permute-start(bf16[4,16,1024]{2,1,0:T(8,128)(2,1)S(1)} %join.1.refs_0_), channel_id=1, source_target_pairs={{0,2},{1,3},{2,0},{3,1},{4,6},{5,7},{6,4},{7,5},{8,10},{9,11},{10,... | collective-permute-start | bytes 393224 | tf_op jit(solution)/shard_map/ppermute | solution.py:265
  77.6 8.4 %collective-permute-start.17 = (bf16[4,16,1024]{2,1,0:T(8,128)(2,1)S(1)}, bf16[4,16,1024]{2,1,0:T(8,128)(2,1)S(1)}, u32[]{:S(2)}, u32[]{:S(2)}) collective-permute-start(bf16[4,16,1024]{2,1,0:T(8,128)(2,1)S(1)} %join.1.refs_0_), channel_id=1, source_target_pairs={{0,1},{1,0},{2,3},{3,2},{4,5},{5,4},{6,7},{7,6},{8,9},{9,8},{10,11... | collective-permute-start | bytes 393224 | tf_op jit(solution)/shard_map/ppermute | solution.py:265
  90.9 6.1 %collective-permute-start.24 = (bf16[8,8192]{1,0:T(8,128)(2,1)S(1)}, bf16[8,8192]{1,0:T(8,128)(2,1)S(1)}, u32[]{:S(2)}, u32[]{:S(2)}) collective-permute-start(bf16[8,8192]{1,0:T(8,128)(2,1)S(1)} %get-tuple-element.37), channel_id=1, source_target_pairs={{0,32},{32,0},{64,96},{96,64},{128,160},{160,128},{192,224},{224,1... | collective-permute-start | bytes 393224 | tf_op jit(solution)/shard_map/ppermute | solution.py:262
  97.0 4.3 %collective-permute-start.25 = (bf16[2,8192]{1,0:T(2,128)(2,1)S(1)}, bf16[2,8192]{1,0:T(2,128)(2,1)S(1)}, u32[]{:S(2)}, u32[]{:S(2)}) collective-permute-start(bf16[2,8192]{1,0:T(2,128)(2,1)S(1)} %get-tuple-element.39), channel_id=1, source_target_pairs={{0,64},{32,96},{64,0},{96,32},{128,192},{160,224},{192,128},{224,1... | collective-permute-start | bytes 98312 | tf_op jit(solution)/shard_map/ppermute | solution.py:262
  97.3 5.7 %collective-permute-start.26 = (bf16[2,8192]{1,0:T(2,128)(2,1)S(1)}, bf16[2,8192]{1,0:T(2,128)(2,1)S(1)}, u32[]{:S(2)}, u32[]{:S(2)}) collective-permute-start(bf16[2,8192]{1,0:T(2,128)(2,1)S(1)} %get-tuple-element.40), channel_id=1, source_target_pairs={{0,128},{32,160},{64,192},{96,224},{128,0},{160,32},{192,64},{224,... | collective-permute-start | bytes 98312 | tf_op jit(solution)/shard_map/ppermute | solution.py:262
  101.4 4.0 %collective-permute-start.27 = (bf16[2,8192]{1,0:T(2,128)(2,1)S(1)}, bf16[2,8192]{1,0:T(2,128)(2,1)S(1)}, u32[]{:S(2)}, u32[]{:S(2)}) collective-permute-start(bf16[2,8192]{1,0:T(2,128)(2,1)S(1)} %get-tuple-element.41), channel_id=1, source_target_pairs={{0,192},{32,224},{64,128},{96,160},{128,64},{160,96},{192,0},{224,... | collective-permute-start | bytes 98312 | tf_op jit(solution)/shard_map/ppermute | solution.py:262
